TPU v7x, 128 devices: a whole 4x4x4 slice. The times are simulated.
128 devices in a mesh: tile: 64 (over z, x, y), view: 2 (over core).
Axes of the slice: x: 4, y: 4, z: 4, core: 2. Of those that a mesh axis runs over, the one named last changes fastest.
Arguments:
- estimate: float32 [1024, 128, 128], P('tile'), may hold values from 0.5 to 2
- view_data: float32 [6, 1024, 128, 128], P('view', 'tile'), may hold values from 0.2 to 5
- psf_taps: float32 [6, 3, 31], P('view'), may hold values from 0.05 to 1
- coverage: int32 [6, 1024], P('view', 'tile'), may hold values 0 or 1
Outputs:
- deconvolved: float32 [1024, 128, 128], P('tile')
All inputs are finite; a program needn't handle non-finite values. No bound on the sum of `coverage` on one device may be relied on, other than what follows from the above.
Results may differ from a plain program's by a relative error of at most 0.00012.
Values sent between devices are 32-bit elements; how exact they have to be, the bound alone decides.
No kernel may reach another device: no remote copies, remote signals or barrier semaphores. Data moves between devices by JAX's collectives and lax.ppermute only.
A program may use at most 128 MiB of HBM per device.

v0:
```python
import functools

import jax
import jax.numpy as jnp
from jax import lax
from jax.experimental import pallas as pl
from jax.experimental.pallas import tpu as pltpu
from jax.sharding import PartitionSpec as P

ITERS = 4
TAPS = 31
REACH = 15
VIEWS = 6
W = 16
HALF = 64
EXT = 96
MID = 80
SLOTS = 48
NZ = 128
PART = 32
OWN_STEP = 65
PART_STEP = 33
F32 = jnp.float32
BF16 = jnp.bfloat16
VMEM = pl.BlockSpec(memory_space=pltpu.VMEM)
SMEM = pl.BlockSpec(memory_space=pltpu.SMEM)


def split(x):
    high = x.astype(BF16)
    return high, (x - high.astype(F32)).astype(BF16)


def dot(a, b):
    return jnp.dot(a, b, preferred_element_type=F32)


def iota(shape, dim):
    return lax.broadcasted_iota(jnp.int32, shape, dim)


def plane_of(slot, odd):
    middle = slot - REACH
    swapped = jnp.where(slot < REACH, slot + W, jnp.where(slot < REACH + W, middle, slot - 46))
    return jnp.where(odd == 0, middle, swapped)


def row_of(j, core):
    first = jnp.where(j < 32, j + 32, jnp.where(j < 64, j - 32, j))
    second = jnp.where(j < 64, j + 64, j - 32)
    return jnp.where(core == 0, first, second)


def mid_row_of(j, core):
    return jnp.where((core == 1) & (j >= 64), j - 16, row_of(j, core))


def put(ref, lead, rows, value):
    high, low = split(value)
    ref[lead + (pl.ds(0, rows),)] = high
    ref[lead + (pl.ds(rows, rows),)] = low


def select(taps, view, axis, index):
    total = jnp.zeros(index.shape, F32)
    for k in range(TAPS):
        total = jnp.where(index == k, taps[(view * 3 + axis) * TAPS + k], total)
    return total


def in_grid(slot, plane, tile):
    at = plane + W * tile
    return (slot < 46) & (at >= 0) & (at < 1024)


def matrices_kernel(where, taps, xf, yf, yt, zf, zt):
    core, tile, odd = where[0], where[1], where[2]

    shape = (VIEWS * W, 2 * SLOTS)
    slot = iota(shape, 1)
    slot = jnp.where(slot < SLOTS, slot, slot - SLOTS)
    plane = plane_of(slot, odd)
    row = iota(shape, 0)
    index = jnp.where(in_grid(slot, plane, tile), plane - row % W + REACH, -1)
    total = jnp.zeros(shape, F32)
    for view in range(VIEWS):
        total = jnp.where(row // W == view, select(taps, view, 0, index), total)
    put(xf, (), VIEWS * W, total)

    def per_view(view, _):
        shape = (MID, 2 * EXT)
        j = iota(shape, 1)
        j = jnp.where(j < EXT, j, j - EXT)
        index = row_of(j, core) - mid_row_of(iota(shape, 0), core) + REACH
        put(yf, (view,), MID, select(taps, view, 1, index))
        shape = (HALF, 2 * MID)
        j = iota(shape, 1)
        j = jnp.where(j < MID, j, j - MID)
        index = row_of(iota(shape, 0), core) - mid_row_of(j, core) + REACH
        put(yt, (view,), HALF, select(taps, view, 1, index))
        difference = iota((NZ, NZ), 0) - iota((NZ, NZ), 1)
        for ref, sign in ((zf, 1), (zt, -1)):
            high, low = split(select(taps, view, 2, sign * difference + REACH))
            for start in (0, NZ):
                ref[view, pl.ds(start, NZ), pl.ds(0, NZ)] = high
                ref[view, pl.ds(start, NZ), pl.ds(NZ, NZ)] = low
        return 0

    lax.fori_loop(0, VIEWS, per_view, 0)


def make_matrices(where, taps):
    shapes = [
        (2 * VIEWS * W, 2 * SLOTS),
        (VIEWS, 2 * MID, 2 * EXT),
        (VIEWS, 2 * HALF, 2 * MID),
        (VIEWS, 2 * NZ, 2 * NZ),
        (VIEWS, 2 * NZ, 2 * NZ),
    ]
    return pl.pallas_call(
        matrices_kernel,
        out_shape=[jax.ShapeDtypeStruct(s, BF16) for s in shapes],
        in_specs=[SMEM, SMEM],
        out_specs=[VMEM] * 5,
        compiler_params=pltpu.CompilerParams(vmem_limit_bytes=6 << 20),
        cost_estimate=pl.CostEstimate(flops=1_000, bytes_accessed=1_000, transcendentals=0),
        name="matrices",
    )(where, taps)


def cover_kernel(where, taps, cover, xt):
    core, tile, odd = where[0], where[1], where[2]
    shape = (SLOTS, 2 * VIEWS * W)
    slot = iota(shape, 0)
    plane = plane_of(slot, odd)
    column = iota(shape, 1)
    column = jnp.where(column < VIEWS * W, column, column - VIEWS * W)
    index = jnp.where(in_grid(slot, plane, tile), plane - column % W + REACH, -1)
    total = jnp.zeros(shape, F32)
    for view in range(VIEWS):
        covered = jnp.zeros((SLOTS, 2 * VIEWS * W), F32)
        for p in range(3 * W):
            covered = jnp.where(plane == p - W, cover[(p // W) * VIEWS * W + view * W + p % W], covered)
        total = jnp.where(column // W == view, select(taps, view, 0, index) * covered, total)
    put(xt, (), SLOTS, total)


def cover_matrix(where, taps, cover):
    return pl.pallas_call(
        cover_kernel,
        out_shape=jax.ShapeDtypeStruct((2 * SLOTS, 2 * VIEWS * W), BF16),
        in_specs=[SMEM, SMEM, SMEM],
        out_specs=VMEM,
        compiler_params=pltpu.CompilerParams(vmem_limit_bytes=2 << 20),
        cost_estimate=pl.CostEstimate(flops=1_000, bytes_accessed=1_000, transcendentals=0),
        name="cover_matrix",
    )(where, taps, cover)


def both(result):
    half = result.shape[0] // 2
    return result[:half] + result[half:]


def pair(result):
    return result[:, :NZ] + result[:, NZ:]


def beside(blocks):
    return jnp.concatenate(blocks, 1)


def along_x(source, target, matrix, rows, taken, given, source_step, target_step):
    group = 16

    def body(step, _):
        parts = [split(source[pl.ds(step * group + i, taken, stride=source_step)]) for i in range(group)]
        operand = jnp.concatenate([beside([p[0] for p in parts]), beside([p[1] for p in parts])], 0)
        result = both(dot(matrix[...], operand))
        for i in range(group):
            target[pl.ds(step * group + i, given, stride=target_step)] = result[:, i * NZ : (i + 1) * NZ]
        return 0

    lax.fori_loop(0, rows // group, body, 0)


def blur_kernel(at, first, own, second, xf, zf, out_high, out_low, ext, mid):
    slot = 0
    for source in (first, own, second):
        for i in range(source.shape[0]):
            ext[pl.ds(slot * PART_STEP, PART)] = source[i, pl.ds(at, PART)]
            slot += 1
    while slot < SLOTS:
        ext[pl.ds(slot * PART_STEP, PART)] = jnp.zeros((PART, NZ), F32)
        slot += 1
    along_x(ext, mid, xf, PART, SLOTS, VIEWS * W, PART_STEP, PART_STEP)

    def along_z(view, _):
        start = pl.multiple_of(view * (W * PART_STEP), 16)
        block = jnp.concatenate([mid[pl.ds(start + i * PART_STEP, PART)] for i in range(W)], 0)
        high, low = split(pair(dot(beside(split(block)), zf[view])))
        for i in range(W):
            out_high[view * W + i] = high[i * PART : (i + 1) * PART]
            out_low[view * W + i] = low[i * PART : (i + 1) * PART]
        return 0

    lax.fori_loop(0, VIEWS, along_z, 0, unroll=3)


def blur(first, own, second, xf, zf, at=0):
    return pl.pallas_call(
        functools.partial(blur_kernel, at),
        out_shape=[jax.ShapeDtypeStruct((VIEWS * W, PART, NZ), BF16)] * 2,
        in_specs=[VMEM] * 5,
        out_specs=[VMEM] * 2,
        scratch_shapes=[pltpu.VMEM((SLOTS * PART_STEP, NZ), F32), pltpu.VMEM((VIEWS * W * PART_STEP, NZ), F32)],
        compiler_params=pltpu.CompilerParams(vmem_limit_bytes=10 << 20),
        cost_estimate=pl.CostEstimate(flops=10_000_000_000, bytes_accessed=3_000_000, transcendentals=0),
        name="blur",
    )(first, own, second, xf, zf)


def correct_kernel(
    near_high, near_low, far_high, far_low, other_high, other_low, mine, theirs, xt, yf, yt, zt,
    near1, near_own, near2, far1, far_own, far2, back, wide,
):
    blurs = ((near_high, far_high, other_high), (near_low, far_low, other_low))

    def inner(data, base, unroll):
        def body(step, _):
            view = base + step
            operand = jnp.concatenate(
                [beside([ref[view * W + i] for i in range(W)]) for refs in blurs for ref in refs], 0
            )
            blurred = both(dot(yf[view], operand))
            measured = beside([data[step, i] for i in range(W)])
            result = both(dot(yt[view], jnp.concatenate(split(measured / blurred), 0)))
            block = jnp.concatenate([result[:, i * NZ : (i + 1) * NZ] for i in range(W)], 0)
            block = pair(dot(beside(split(block)), zt[view]))
            start = pl.multiple_of(view * (W * OWN_STEP), 16)
            for i in range(W):
                back[pl.ds(start + i * OWN_STEP, HALF)] = block[i * HALF : (i + 1) * HALF]
            return 0

        lax.fori_loop(0, VIEWS // 2, body, 0, unroll=unroll)

    inner(mine, 0, 3)
    inner(theirs, VIEWS // 2, 1)
    along_x(back, wide, xt, HALF, VIEWS * W, SLOTS, OWN_STEP, OWN_STEP)
    for at, outs in ((0, (near1, near_own, near2)), (PART, (far1, far_own, far2))):
        for slot, out in zip((0, 15, 31), outs):
            for i in range(out.shape[0]):
                out[i] = wide[pl.ds((slot + i) * OWN_STEP + at, PART)]


PARTS = [(15, PART, NZ), (16, PART, NZ), (15, PART, NZ)]


def correct(blurs, mine, theirs, xt, yf, yt, zt):
    return pl.pallas_call(
        correct_kernel,
        out_shape=[jax.ShapeDtypeStruct(s, F32) for s in PARTS * 2],
        in_specs=[VMEM] * 12,
        out_specs=[VMEM] * 6,
        scratch_shapes=[
            pltpu.VMEM((VIEWS * W * OWN_STEP, NZ), F32),
            pltpu.VMEM((SLOTS * OWN_STEP, NZ), F32),
        ],
        compiler_params=pltpu.CompilerParams(vmem_limit_bytes=26 << 20),
        cost_estimate=pl.CostEstimate(flops=4_000_000_000, bytes_accessed=16_000_000, transcendentals=0),
        name="correct",
    )(*blurs, mine, theirs, xt, yf, yt, zt)


def begin_kernel(where, estimate, current, send1, send2):
    core, odd = where[0], where[2]
    for start, at in ((32 + 32 * core, 0), (96 * core, PART)):
        rows = pl.ds(pl.multiple_of(start, 32), PART)
        for i in range(W):
            current[i, pl.ds(at, PART)] = estimate[i, rows]
    send1[...] = current[pl.ds(odd, 15)]
    send2[...] = current[pl.ds(1 - odd, 15)]


def begin(where, estimate):
    shapes = [(16, HALF, NZ), (15, HALF, NZ), (15, HALF, NZ)]
    return pl.pallas_call(
        begin_kernel,
        out_shape=[jax.ShapeDtypeStruct(s, F32) for s in shapes],
        in_specs=[SMEM, VMEM],
        out_specs=[VMEM] * 3,
        compiler_params=pltpu.CompilerParams(vmem_limit_bytes=6 << 20),
        cost_estimate=pl.CostEstimate(flops=1_000, bytes_accessed=1_000, transcendentals=0),
        name="begin",
    )(where, estimate)


def rows_kernel(where, data, mine, send):
    core = where[0]
    for ref, who in ((mine, core), (send, 1 - core)):
        for start, at, count in ((32 + 32 * who, 0, 32), (96 * who, 32, 32), (64 - 16 * who, 64, 16)):
            source = pl.ds(pl.multiple_of(start, 16), count)
            for view in range(VIEWS // 2):
                for i in range(W):
                    ref[view, i, pl.ds(at, count)] = data[view, i, source]


def rows(where, data):
    return pl.pallas_call(
        rows_kernel,
        out_shape=[jax.ShapeDtypeStruct((VIEWS // 2, W, MID, NZ), F32)] * 2,
        in_specs=[SMEM, VMEM],
        out_specs=[VMEM] * 2,
        compiler_params=pltpu.CompilerParams(vmem_limit_bytes=10 << 20),
        cost_estimate=pl.CostEstimate(flops=1_000, bytes_accessed=1_000, transcendentals=0),
        name="rows",
    )(where, data)


def add_neighbours(where, keep, scale, current, total, from1, from2, new, work):
    odd = where[2]
    work[...] = total[...]
    work[pl.ds(odd, 15)] += from1[...]
    work[pl.ds(1 - odd, 15)] += from2[...]
    for i in range(W):
        new[i] = current[i] * (work[i] + keep[i]) * scale[i]


def update_kernel(where, keep, scale, current, total, from1, from2, new, send1, send2, work):
    odd = where[2]
    add_neighbours(where, keep, scale, current, total, from1, from2, new, work)
    send1[...] = new[pl.ds(odd, 15)]
    send2[...] = new[pl.ds(1 - odd, 15)]


def update(where, keep, scale, current, total, from1, from2, last):
    shapes = [PARTS[1]] if last else [PARTS[1], PARTS[0], PARTS[2]]
    return pl.pallas_call(
        add_neighbours if last else update_kernel,
        out_shape=[jax.ShapeDtypeStruct(s, F32) for s in shapes],
        in_specs=[SMEM] * 3 + [VMEM] * 4,
        out_specs=[VMEM] * len(shapes),
        scratch_shapes=[pltpu.VMEM(PARTS[1], F32)],
        compiler_params=pltpu.CompilerParams(vmem_limit_bytes=4 << 20),
        cost_estimate=pl.CostEstimate(flops=1_000_000, bytes_accessed=2_000_000, transcendentals=0),
        name="update",
    )(where, keep, scale, current, total, from1, from2)


def exchange(x, odd, tiles):
    pairs = []
    for t in range(odd, tiles, 2):
        pairs += [(t, (t + 1) % tiles), ((t + 1) % tiles, t)]
    return lax.ppermute(x, "tile", pairs)


def swap(x):
    return lax.ppermute(x, "view", [(0, 1), (1, 0)])


def per_device(estimate, view_data, psf_taps, coverage):
    tiles = lax.axis_size("tile")
    core = lax.axis_index("view")
    tile = lax.axis_index("tile")
    where = jnp.stack([core, tile, tile % 2]).astype(jnp.int32)
    current, send1, send2 = begin(where, estimate)
    other_current = swap(current)
    psf_taps, coverage, send1, send2 = lax.optimization_barrier((psf_taps, coverage, send1, send2))

    norm_taps = psf_taps / jnp.sum(psf_taps, axis=-1, keepdims=True)
    own = jnp.concatenate([norm_taps.reshape(-1), coverage.astype(F32).reshape(-1)])
    other, view_data = lax.optimization_barrier((swap(own), view_data))
    count = norm_taps.size
    taps = jnp.concatenate([own[:count], other[:count]])
    cover = jnp.concatenate([own[count:], other[count:]])
    ring = [(i, (i + 1) % tiles) for i in range(tiles)]
    before = lax.ppermute(cover, "tile", ring)
    after = lax.ppermute(cover, "tile", [(j, i) for i, j in ring])
    seen = jnp.sum(cover.reshape(VIEWS, W), axis=0)
    keep = 1.0 - jnp.minimum(seen, 1.0)
    scale = 1.0 / jnp.maximum(seen, 1.0)
    mine, theirs = rows(where, view_data)
    theirs = swap(theirs)
    xf, yf, yt, zf, zt = make_matrices(where, taps)
    xt = cover_matrix(where, taps, jnp.concatenate([before, cover, after]))

    for iteration in range(ITERS):
        last = iteration == ITERS - 1
        if iteration == 0:
            send1, send2 = exchange(send1, 1, tiles), exchange(send2, 0, tiles)
            others = blur(swap(send1), other_current, swap(send2), xf, zf)
            blurs = blur(send1, current, send2, xf, zf) + blur(send1, current, send2, xf, zf, PART)
            near, far = current[:, :PART], current[:, PART:]
        else:
            near1, near2 = exchange(near1, 1, tiles), exchange(near2, 0, tiles)
            far1, far2 = exchange(far1, 1, tiles), exchange(far2, 0, tiles)
            blurs = blur(near1, near, near2, xf, zf)
            others = blur(swap(near1), swap(near), swap(near2), xf, zf)
            far, others = lax.optimization_barrier((far, others))
            blurs = blurs + blur(far1, far, far2, xf, zf)
        near1, near_total, near2, far1, far_total, far2 = correct(blurs + others, mine, theirs, xt, yf, yt, zt)
        near1, near2 = exchange(near1, 1, tiles), exchange(near2, 0, tiles)
        far1, far2 = exchange(far1, 1, tiles), exchange(far2, 0, tiles)
        near, *sends = update(where, keep, scale, near, near_total, near1, near2, last)
        if not last:
            near1, near2 = sends
        far1, far2, near = lax.optimization_barrier((far1, far2, near))
        far, *sends = update(where, keep, scale, far, far_total, far1, far2, last)
        if not last:
            far1, far2 = sends

    zero = core == 0
    other_near, other_far = swap(near), swap(far)
    return jnp.concatenate(
        [
            jnp.where(zero, far, other_far),
            jnp.where(zero, near, other_near),
            jnp.where(zero, other_near, near),
            jnp.where(zero, other_far, far),
        ],
        1,
    )


def solution(mesh):
    return jax.shard_map(
        per_device,
        mesh=mesh,
        in_specs=(
            P("tile", None, None),
            P("view", "tile", None, None),
            P("view", None, None),
            P("view", "tile"),
        ),
        out_specs=P("tile", None, None),
        check_vma=False,
    )
```

profile of v0, /device:TPU:1, one launch (start us, length us, event | category | flops | bytes accessed | tf_op | source)
XLA Modules:
  0.0 187.4 jit_solution(1380812387204709745)
XLA Ops:
  1.3 1.6 begin.1
  6.1 8.5 %collective-permute-start.1 = (f32[15,64,128]{2,1,0:T(8,128)}, f32[15,64,128]{2,1,0:T(8,128)S(1)}, u32[]{:S(2)}, u32[]{:S(2)}) collective-permute-start(f32[15,64,128]{2,1,0:T(8,128)} %get-tuple-element.114), channel_id=1, source_target_pairs={{2,4},{4,2},{6,8},{8,6},{10,12},{12,10},{14,16},{16,14},{18,20},{2... | collective-permute-start | bytes 1474568 | tf_op jit(solution)/shard_map/ppermute | solution.py:354
  15.1 1.7 collective-permute-start.7
  16.9 5.2 %collective-permute-start.8 = (f32[96]{0:T(128)S(1)}, f32[96]{0:T(128)S(1)}, u32[]{:S(2)}, u32[]{:S(2)}) collective-permute-start(f32[96]{0:T(128)S(1)} %pad_maximum_fusion.4), channel_id=1, source_target_pairs={{2,0},{4,2},{6,4},{8,6},{10,8},{12,10},{14,12},{16,14},{18,16},{20... | collective-permute-start | bytes 1160 | tf_op jit(solution)/shard_map/ppermute | solution.py:378
  22.1 4.8 %matrices.1 = (bf16[192,96]{1,0:T(8,128)(2,1)S(1)}, bf16[6,160,192]{2,1,0:T(8,128)(2,1)S(1)}, bf16[6,128,160]{2,1,0:T(8,128)(2,1)S(1)}, bf16[6,256,256]{2,1,0:T(8,128)(2,1)S(1)}, bf16[6,256,256]{2,1,0:T(8,128)(2,1)S(1)}) custom-call(s32[3]{0:T(128)S(1)} %pad_add_fusion.where, f32[558]{0:T(1024)S(1)} %pad_maximum_fusion.1.taps), custom_call_target="tpu_custom_call" | custom-call | flops 1000 | bytes 1000 | tf_op jit(solution)/shard_map/matrices/pallas_call | solution.py:120
  27.0 1.9 %copy-done = f32[3,16,128,128]{3,2,1,0:T(8,128)S(1)} copy-done((f32[3,16,128,128]{3,2,1,0:T(8,128)S(1)}, f32[3,16,128,128]{3,2,1,0:T(8,128)}, u32[]{:S(2)}) %copy-start) | copy-done | bytes 3145752
  30.5 1.6 cover_matrix.1.xt
  35.8 1.5 blur.14
  37.4 5.9 %correct.4 = (f32[15,32,128]{2,1,0:T(8,128)}, f32[16,32,128]{2,1,0:T(8,128)S(1)}, f32[15,32,128]{2,1,0:T(8,128)}, f32[15,32,128]{2,1,0:T(8,128)S(1)}, f32[16,32,...) custom-call(bf16[96,32,128]{2,1,0:T(8,128)(2,1)S(1)} %get-tuple-element.118.near_high, ...), custom_call_target="tpu_custom_call" | custom-call | flops 4000000000 | bytes 16000000 | tf_op jit(solution)/shard_map/correct/pallas_call | solution.py:260
  44.0 3.5 %collective-permute-start.11 = (f32[15,32,128]{2,1,0:T(8,128)}, f32[15,32,128]{2,1,0:T(8,128)S(1)}, u32[]{:S(2)}, u32[]{:S(2)}) collective-permute-start(f32[15,32,128]{2,1,0:T(8,128)} %get-tuple-element.134), channel_id=1, source_target_pairs={{2,4},{4,2},{6,8},{8,6},{10,12},{12,10},{14,16},{16,14},{18,20},{2... | collective-permute-start | bytes 737288 | tf_op jit(solution)/shard_map/ppermute | solution.py:354
  47.7 1.5 collective-permute-start.10
  49.2 3.4 %collective-permute-start.9 = (f32[15,32,128]{2,1,0:T(8,128)S(1)}, f32[15,32,128]{2,1,0:T(8,128)S(1)}, u32[]{:S(2)}, u32[]{:S(2)}) collective-permute-start(f32[15,32,128]{2,1,0:T(8,128)S(1)} %get-tuple-element.131), channel_id=1, source_target_pairs={{2,4},{4,2},{6,8},{8,6},{10,12},{12,10},{14,16},{16,14},{18,20},{2... | collective-permute-start | bytes 737288 | tf_op jit(solution)/shard_map/ppermute | solution.py:354
  52.6 4.5 %collective-permute-done.11.from1 = f32[15,32,128]{2,1,0:T(8,128)S(1)} collective-permute-done((f32[15,32,128]{2,1,0:T(8,128)}, f32[15,32,128]{2,1,0:T(8,128)S(1)}, u32[]{:S(2)}, u32[]{:S(2)}) %collective-permute-start.11) | collective-permute-done | bytes 245792 | tf_op jit(solution)/shard_map/ppermute | solution.py:354
  57.8 3.6 %collective-permute-start.13 = (f32[15,32,128]{2,1,0:T(8,128)S(1)}, f32[15,32,128]{2,1,0:T(8,128)S(1)}, u32[]{:S(2)}, u32[]{:S(2)}) collective-permute-start(f32[15,32,128]{2,1,0:T(8,128)S(1)} %get-tuple-element.140), channel_id=1, source_target_pairs={{2,4},{4,2},{6,8},{8,6},{10,12},{12,10},{14,16},{16,14},{18,20},{2... | collective-permute-start | bytes 737288 | tf_op jit(solution)/shard_map/ppermute | solution.py:354
  61.7 1.6 collective-permute-start.15
  64.0 3.8 %collective-permute-start.18 = (f32[15,32,128]{2,1,0:T(8,128)S(1)}, f32[15,32,128]{2,1,0:T(8,128)S(1)}, u32[]{:S(2)}, u32[]{:S(2)}) collective-permute-start(f32[15,32,128]{2,1,0:T(8,128)S(1)} %get-tuple-element.148), channel_id=1, source_target_pairs={{2,4},{4,2},{6,8},{8,6},{10,12},{12,10},{14,16},{16,14},{18,20},{2... | collective-permute-start | bytes 737288 | tf_op jit(solution)/shard_map/ppermute | solution.py:354
  67.8 1.8 collective-permute-done.13.first
  69.6 2.1 %collective-permute-start.14 = (f32[15,32,128]{2,1,0:T(8,128)S(1)}, f32[15,32,128]{2,1,0:T(8,128)S(1)}, u32[]{:S(2)}, u32[]{:S(2)}) collective-permute-start(f32[15,32,128]{2,1,0:T(8,128)S(1)} %collective-permute-done.13.first), channel_id=1, source_target_pairs={{0,1},{1,0},{2,3},{3,2},{4,5},{5,4},{6,7},{7,6},{8,9},{9,8},{10,11... | collective-permute-start | bytes 737288 | tf_op jit(solution)/shard_map/ppermute | solution.py:358
  73.2 1.5 blur.15
  74.8 2.5 %collective-permute-done.18.first = f32[15,32,128]{2,1,0:T(8,128)S(1)} collective-permute-done((f32[15,32,128]{2,1,0:T(8,128)S(1)}, f32[15,32,128]{2,1,0:T(8,128)S(1)}, u32[]{:S(2)}, u32[]{:S(2)}) %collective-permute-start.18) | collective-permute-done | bytes 245792 | tf_op jit(solution)/shard_map/ppermute | solution.py:354
  77.3 1.5 blur.17
  78.9 5.3 %correct.5 = (f32[15,32,128]{2,1,0:T(8,128)S(1)}, f32[16,32,128]{2,1,0:T(8,128)S(1)}, f32[15,32,128]{2,1,0:T(8,128)S(1)}, f32[15,32,128]{2,1,0:T(8,128)S(1)}, f3...) custom-call(bf16[96,32,128]{2,1,0:T(8,128)(2,1)S(1)} %get-tuple-element.146.near_high, ...), custom_call_target="tpu_custom_call" | custom-call | flops 4000000000 | bytes 16000000 | tf_op jit(solution)/shard_map/correct/pallas_call | solution.py:260
  84.1 3.6 %collective-permute-start.22 = (f32[15,32,128]{2,1,0:T(8,128)S(1)}, f32[15,32,128]{2,1,0:T(8,128)S(1)}, u32[]{:S(2)}, u32[]{:S(2)}) collective-permute-start(f32[15,32,128]{2,1,0:T(8,128)S(1)} %get-tuple-element.158), channel_id=1, source_target_pairs={{2,4},{4,2},{6,8},{8,6},{10,12},{12,10},{14,16},{16,14},{18,20},{2... | collective-permute-start | bytes 737288 | tf_op jit(solution)/shard_map/ppermute | solution.py:354
  87.8 3.4 %collective-permute-start.20 = (f32[15,32,128]{2,1,0:T(8,128)S(1)}, f32[15,32,128]{2,1,0:T(8,128)S(1)}, u32[]{:S(2)}, u32[]{:S(2)}) collective-permute-start(f32[15,32,128]{2,1,0:T(8,128)S(1)} %get-tuple-element.155), channel_id=1, source_target_pairs={{2,4},{4,2},{6,8},{8,6},{10,12},{12,10},{14,16},{16,14},{18,20},{2... | collective-permute-start | bytes 737288 | tf_op jit(solution)/shard_map/ppermute | solution.py:354
  91.1 5.2 %collective-permute-done.22.from1 = f32[15,32,128]{2,1,0:T(8,128)S(1)} collective-permute-done((f32[15,32,128]{2,1,0:T(8,128)S(1)}, f32[15,32,128]{2,1,0:T(8,128)S(1)}, u32[]{:S(2)}, u32[]{:S(2)}) %collective-permute-start.22) | collective-permute-done | bytes 245792 | tf_op jit(solution)/shard_map/ppermute | solution.py:354
  97.1 3.6 %collective-permute-start.24 = (f32[15,32,128]{2,1,0:T(8,128)S(1)}, f32[15,32,128]{2,1,0:T(8,128)S(1)}, u32[]{:S(2)}, u32[]{:S(2)}) collective-permute-start(f32[15,32,128]{2,1,0:T(8,128)S(1)} %get-tuple-element.164), channel_id=1, source_target_pairs={{2,4},{4,2},{6,8},{8,6},{10,12},{12,10},{14,16},{16,14},{18,20},{2... | collective-permute-start | bytes 737288 | tf_op jit(solution)/shard_map/ppermute | solution.py:354
  101.6 2.4 %collective-permute-start.26 = (f32[16,32,128]{2,1,0:T(8,128)S(1)}, f32[16,32,128]{2,1,0:T(8,128)S(1)}, u32[]{:S(2)}, u32[]{:S(2)}) collective-permute-start(f32[16,32,128]{2,1,0:T(8,128)S(1)} %get-tuple-element.165.own.current), channel_id=1, source_target_pairs={{0,1},{1,0},{2,3},{3,2},{4,5},{5,4},{6,7},{7,6},{8,9},{9,8},{10,11... | collective-permute-start | bytes 786440 | tf_op jit(solution)/shard_map/ppermute | solution.py:358
  104.7 3.5 %collective-permute-start.29 = (f32[15,32,128]{2,1,0:T(8,128)S(1)}, f32[15,32,128]{2,1,0:T(8,128)S(1)}, u32[]{:S(2)}, u32[]{:S(2)}) collective-permute-start(f32[15,32,128]{2,1,0:T(8,128)S(1)} %get-tuple-element.172), channel_id=1, source_target_pairs={{2,4},{4,2},{6,8},{8,6},{10,12},{12,10},{14,16},{16,14},{18,20},{2... | collective-permute-start | bytes 737288 | tf_op jit(solution)/shard_map/ppermute | solution.py:354
  108.1 3.6 %collective-permute-start.25 = (f32[15,32,128]{2,1,0:T(8,128)S(1)}, f32[15,32,128]{2,1,0:T(8,128)S(1)}, u32[]{:S(2)}, u32[]{:S(2)}) collective-permute-start(f32[15,32,128]{2,1,0:T(8,128)S(1)} %collective-permute-done.24.first), channel_id=1, source_target_pairs={{0,1},{1,0},{2,3},{3,2},{4,5},{5,4},{6,7},{7,6},{8,9},{9,8},{10,11... | collective-permute-start | bytes 737288 | tf_op jit(solution)/shard_map/ppermute | solution.py:358
  113.3 1.5 blur.18
  114.8 2.9 %collective-permute-done.29.first = f32[15,32,128]{2,1,0:T(8,128)S(1)} collective-permute-done((f32[15,32,128]{2,1,0:T(8,128)S(1)}, f32[15,32,128]{2,1,0:T(8,128)S(1)}, u32[]{:S(2)}, u32[]{:S(2)}) %collective-permute-start.29) | collective-permute-done | bytes 245792 | tf_op jit(solution)/shard_map/ppermute | solution.py:354
  117.8 1.5 blur.20
  119.3 5.3 %correct.6 = (f32[15,32,128]{2,1,0:T(8,128)S(1)}, f32[16,32,128]{2,1,0:T(8,128)S(1)}, f32[15,32,128]{2,1,0:T(8,128)S(1)}, f32[15,32,128]{2,1,0:T(8,128)S(1)}, f3...) custom-call(bf16[96,32,128]{2,1,0:T(8,128)(2,1)S(1)} %get-tuple-element.170.near_high, ...), custom_call_target="tpu_custom_call" | custom-call | flops 4000000000 | bytes 16000000 | tf_op jit(solution)/shard_map/correct/pallas_call | solution.py:260
  124.6 3.4 %collective-permute-start.33 = (f32[15,32,128]{2,1,0:T(8,128)S(1)}, f32[15,32,128]{2,1,0:T(8,128)S(1)}, u32[]{:S(2)}, u32[]{:S(2)}) collective-permute-start(f32[15,32,128]{2,1,0:T(8,128)S(1)} %get-tuple-element.182), channel_id=1, source_target_pairs={{2,4},{4,2},{6,8},{8,6},{10,12},{12,10},{14,16},{16,14},{18,20},{2... | collective-permute-start | bytes 737288 | tf_op jit(solution)/shard_map/ppermute | solution.py:354
  128.0 3.5 %collective-permute-start.31 = (f32[15,32,128]{2,1,0:T(8,128)S(1)}, f32[15,32,128]{2,1,0:T(8,128)S(1)}, u32[]{:S(2)}, u32[]{:S(2)}) collective-permute-start(f32[15,32,128]{2,1,0:T(8,128)S(1)} %get-tuple-element.179), channel_id=1, source_target_pairs={{2,4},{4,2},{6,8},{8,6},{10,12},{12,10},{14,16},{16,14},{18,20},{2... | collective-permute-start | bytes 737288 | tf_op jit(solution)/shard_map/ppermute | solution.py:354
  131.6 5.2 %collective-permute-done.33.from1 = f32[15,32,128]{2,1,0:T(8,128)S(1)} collective-permute-done((f32[15,32,128]{2,1,0:T(8,128)S(1)}, f32[15,32,128]{2,1,0:T(8,128)S(1)}, u32[]{:S(2)}, u32[]{:S(2)}) %collective-permute-start.33) | collective-permute-done | bytes 245792 | tf_op jit(solution)/shard_map/ppermute | solution.py:354
  137.5 3.4 %collective-permute-start.35 = (f32[15,32,128]{2,1,0:T(8,128)S(1)}, f32[15,32,128]{2,1,0:T(8,128)S(1)}, u32[]{:S(2)}, u32[]{:S(2)}) collective-permute-start(f32[15,32,128]{2,1,0:T(8,128)S(1)} %get-tuple-element.188), channel_id=1, source_target_pairs={{2,4},{4,2},{6,8},{8,6},{10,12},{12,10},{14,16},{16,14},{18,20},{2... | collective-permute-start | bytes 737288 | tf_op jit(solution)/shard_map/ppermute | solution.py:354
  142.0 2.2 %collective-permute-start.37 = (f32[16,32,128]{2,1,0:T(8,128)S(1)}, f32[16,32,128]{2,1,0:T(8,128)S(1)}, u32[]{:S(2)}, u32[]{:S(2)}) collective-permute-start(f32[16,32,128]{2,1,0:T(8,128)S(1)} %get-tuple-element.189.own.current), channel_id=1, source_target_pairs={{0,1},{1,0},{2,3},{3,2},{4,5},{5,4},{6,7},{7,6},{8,9},{9,8},{10,11... | collective-permute-start | bytes 786440 | tf_op jit(solution)/shard_map/ppermute | solution.py:358
  145.0 3.6 %collective-permute-start.40 = (f32[15,32,128]{2,1,0:T(8,128)S(1)}, f32[15,32,128]{2,1,0:T(8,128)S(1)}, u32[]{:S(2)}, u32[]{:S(2)}) collective-permute-start(f32[15,32,128]{2,1,0:T(8,128)S(1)} %get-tuple-element.196), channel_id=1, source_target_pairs={{2,4},{4,2},{6,8},{8,6},{10,12},{12,10},{14,16},{16,14},{18,20},{2... | collective-permute-start | bytes 737288 | tf_op jit(solution)/shard_map/ppermute | solution.py:354
  148.6 3.6 %collective-permute-start.36 = (f32[15,32,128]{2,1,0:T(8,128)S(1)}, f32[15,32,128]{2,1,0:T(8,128)S(1)}, u32[]{:S(2)}, u32[]{:S(2)}) collective-permute-start(f32[15,32,128]{2,1,0:T(8,128)S(1)} %collective-permute-done.35.first), channel_id=1, source_target_pairs={{0,1},{1,0},{2,3},{3,2},{4,5},{5,4},{6,7},{7,6},{8,9},{9,8},{10,11... | collective-permute-start | bytes 737288 | tf_op jit(solution)/shard_map/ppermute | solution.py:358
  153.7 1.5 blur.21
  155.3 2.8 %collective-permute-done.40.first = f32[15,32,128]{2,1,0:T(8,128)S(1)} collective-permute-done((f32[15,32,128]{2,1,0:T(8,128)S(1)}, f32[15,32,128]{2,1,0:T(8,128)S(1)}, u32[]{:S(2)}, u32[]{:S(2)}) %collective-permute-start.40) | collective-permute-done | bytes 245792 | tf_op jit(solution)/shard_map/ppermute | solution.py:354
  159.6 5.3 %correct.7 = (f32[15,32,128]{2,1,0:T(8,128)S(1)}, f32[16,32,128]{2,1,0:T(8,128)S(1)}, f32[15,32,128]{2,1,0:T(8,128)S(1)}, f32[15,32,128]{2,1,0:T(8,128)S(1)}, f3...) custom-call(bf16[96,32,128]{2,1,0:T(8,128)(2,1)S(1)} %get-tuple-element.194.near_high, ...), custom_call_target="tpu_custom_call" | custom-call | flops 4000000000 | bytes 16000000 | tf_op jit(solution)/shard_map/correct/pallas_call | solution.py:260
  164.9 3.6 %collective-permute-start.44 = (f32[15,32,128]{2,1,0:T(8,128)S(1)}, f32[15,32,128]{2,1,0:T(8,128)S(1)}, u32[]{:S(2)}, u32[]{:S(2)}) collective-permute-start(f32[15,32,128]{2,1,0:T(8,128)S(1)} %get-tuple-element.206), channel_id=1, source_target_pairs={{2,4},{4,2},{6,8},{8,6},{10,12},{12,10},{14,16},{16,14},{18,20},{2... | collective-permute-start | bytes 737288 | tf_op jit(solution)/shard_map/ppermute | solution.py:354
  168.5 3.4 %collective-permute-start.42 = (f32[15,32,128]{2,1,0:T(8,128)S(1)}, f32[15,32,128]{2,1,0:T(8,128)S(1)}, u32[]{:S(2)}, u32[]{:S(2)}) collective-permute-start(f32[15,32,128]{2,1,0:T(8,128)S(1)} %get-tuple-element.203), channel_id=1, source_target_pairs={{2,4},{4,2},{6,8},{8,6},{10,12},{12,10},{14,16},{16,14},{18,20},{2... | collective-permute-start | bytes 737288 | tf_op jit(solution)/shard_map/ppermute | solution.py:354
  171.9 5.2 %collective-permute-done.44.from1 = f32[15,32,128]{2,1,0:T(8,128)S(1)} collective-permute-done((f32[15,32,128]{2,1,0:T(8,128)S(1)}, f32[15,32,128]{2,1,0:T(8,128)S(1)}, u32[]{:S(2)}, u32[]{:S(2)}) %collective-permute-start.44) | collective-permute-done | bytes 245792 | tf_op jit(solution)/shard_map/ppermute | solution.py:354
  177.7 4.6 %collective-permute-done.42.from1 = f32[15,32,128]{2,1,0:T(8,128)S(1)} collective-permute-done((f32[15,32,128]{2,1,0:T(8,128)S(1)}, f32[15,32,128]{2,1,0:T(8,128)S(1)}, u32[]{:S(2)}, u32[]{:S(2)}) %collective-permute-start.42) | collective-permute-done | bytes 245792 | tf_op jit(solution)/shard_map/ppermute | solution.py:354
  182.3 1.7 collective-permute-start.47
  (118 shorter events, 28.0 us)
Async XLA Ops:
  4.7 10.3 %collective-permute-start = (f32[327]{0:T(512)S(1)}, f32[327]{0:T(512)S(1)}, u32[]{:S(2)}, u32[]{:S(2)}) collective-permute-start(f32[327]{0:T(512)S(1)} %pad_maximum_fusion.2), channel_id=1, source_target_pairs={{0,1},{1,0},{2,3},{3,2},{4,5},{5,4},{6,7},{7,6},{8,9},{9,8},{10,11... | collective-permute-start | bytes 3932 | tf_op jit(solution)/shard_map/ppermute | solution.py:358
  6.1 26.0 %collective-permute-start.1 = (f32[15,64,128]{2,1,0:T(8,128)}, f32[15,64,128]{2,1,0:T(8,128)S(1)}, u32[]{:S(2)}, u32[]{:S(2)}) collective-permute-start(f32[15,64,128]{2,1,0:T(8,128)} %get-tuple-element.114), channel_id=1, source_target_pairs={{2,4},{4,2},{6,8},{8,6},{10,12},{12,10},{14,16},{16,14},{18,20},{2... | collective-permute-start | bytes 1474568 | tf_op jit(solution)/shard_map/ppermute | solution.py:354
  14.6 17.6 %collective-permute-start.2 = (f32[15,64,128]{2,1,0:T(8,128)}, f32[15,64,128]{2,1,0:T(8,128)S(1)}, u32[]{:S(2)}, u32[]{:S(2)}) collective-permute-start(f32[15,64,128]{2,1,0:T(8,128)} %get-tuple-element.115), channel_id=1, source_target_pairs={{0,2},{2,0},{4,6},{6,4},{8,10},{10,8},{12,14},{14,12},{16,18},{18,... | collective-permute-start | bytes 1474568 | tf_op jit(solution)/shard_map/ppermute | solution.py:354
  14.6 21.1 %collective-permute-start.4 = (f32[16,64,128]{2,1,0:T(8,128)S(1)}, f32[16,64,128]{2,1,0:T(8,128)S(1)}, u32[]{:S(2)}, u32[]{:S(2)}) collective-permute-start(f32[16,64,128]{2,1,0:T(8,128)S(1)} %get-tuple-element.113.own), channel_id=1, source_target_pairs={{0,1},{1,0},{2,3},{3,2},{4,5},{5,4},{6,7},{7,6},{8,9},{9,8},{10,11... | collective-permute-start | bytes 1572872 | tf_op jit(solution)/shard_map/ppermute | solution.py:358
  15.1 14.6 %collective-permute-start.7 = (f32[96]{0:T(128)S(1)}, f32[96]{0:T(128)S(1)}, u32[]{:S(2)}, u32[]{:S(2)}) collective-permute-start(f32[96]{0:T(128)S(1)} %pad_maximum_fusion.4), channel_id=1, source_target_pairs={{0,2},{2,4},{4,6},{6,8},{8,10},{10,12},{12,14},{14,16},{16,18},{18... | collective-permute-start | bytes 1160 | tf_op jit(solution)/shard_map/ppermute | solution.py:377
  16.9 12.8 %collective-permute-start.8 = (f32[96]{0:T(128)S(1)}, f32[96]{0:T(128)S(1)}, u32[]{:S(2)}, u32[]{:S(2)}) collective-permute-start(f32[96]{0:T(128)S(1)} %pad_maximum_fusion.4), channel_id=1, source_target_pairs={{2,0},{4,2},{6,4},{8,6},{10,8},{12,10},{14,12},{16,14},{18,16},{20... | collective-permute-start | bytes 1160 | tf_op jit(solution)/shard_map/ppermute | solution.py:378
  29.8 7.5 %collective-permute-start.6 = (f32[3,16,80,128]{3,2,1,0:T(8,128)S(1)}, f32[3,16,80,128]{3,2,1,0:T(8,128)S(1)}, u32[]{:S(2)}, u32[]{:S(2)}) collective-permute-start(f32[3,16,80,128]{3,2,1,0:T(8,128)S(1)} %get-tuple-element.126), channel_id=1, source_target_pairs={{0,1},{1,0},{2,3},{3,2},{4,5},{5,4},{6,7},{7,6},{8,9},{9,8},{10,11... | collective-permute-start | bytes 5898248 | tf_op jit(solution)/shard_map/ppermute | solution.py:358
  32.1 3.7 %collective-permute-start.3 = (f32[15,64,128]{2,1,0:T(8,128)S(1)}, f32[15,64,128]{2,1,0:T(8,128)S(1)}, u32[]{:S(2)}, u32[]{:S(2)}) collective-permute-start(f32[15,64,128]{2,1,0:T(8,128)S(1)} %collective-permute-done.1.first), channel_id=1, source_target_pairs={{0,1},{1,0},{2,3},{3,2},{4,5},{5,4},{6,7},{7,6},{8,9},{9,8},{10,11... | collective-permute-start | bytes 1474568 | tf_op jit(solution)/shard_map/ppermute | solution.py:358
  32.2 3.6 %collective-permute-start.5 = (f32[15,64,128]{2,1,0:T(8,128)S(1)}, f32[15,64,128]{2,1,0:T(8,128)S(1)}, u32[]{:S(2)}, u32[]{:S(2)}) collective-permute-start(f32[15,64,128]{2,1,0:T(8,128)S(1)} %collective-permute-done.2.second), channel_id=1, source_target_pairs={{0,1},{1,0},{2,3},{3,2},{4,5},{5,4},{6,7},{7,6},{8,9},{9,8},{10,11... | collective-permute-start | bytes 1474568 | tf_op jit(solution)/shard_map/ppermute | solution.py:358
  44.0 13.1 %collective-permute-start.11 = (f32[15,32,128]{2,1,0:T(8,128)}, f32[15,32,128]{2,1,0:T(8,128)S(1)}, u32[]{:S(2)}, u32[]{:S(2)}) collective-permute-start(f32[15,32,128]{2,1,0:T(8,128)} %get-tuple-element.134), channel_id=1, source_target_pairs={{2,4},{4,2},{6,8},{8,6},{10,12},{12,10},{14,16},{16,14},{18,20},{2... | collective-permute-start | bytes 737288 | tf_op jit(solution)/shard_map/ppermute | solution.py:354
  47.5 9.5 %collective-permute-start.12 = (f32[15,32,128]{2,1,0:T(8,128)}, f32[15,32,128]{2,1,0:T(8,128)S(1)}, u32[]{:S(2)}, u32[]{:S(2)}) collective-permute-start(f32[15,32,128]{2,1,0:T(8,128)} %get-tuple-element.135), channel_id=1, source_target_pairs={{0,2},{2,0},{4,6},{6,4},{8,10},{10,8},{12,14},{14,12},{16,18},{18,... | collective-permute-start | bytes 737288 | tf_op jit(solution)/shard_map/ppermute | solution.py:354
  47.7 13.7 %collective-permute-start.10 = (f32[15,32,128]{2,1,0:T(8,128)}, f32[15,32,128]{2,1,0:T(8,128)S(1)}, u32[]{:S(2)}, u32[]{:S(2)}) collective-permute-start(f32[15,32,128]{2,1,0:T(8,128)} %copy-done.10), channel_id=1, source_target_pairs={{0,2},{2,0},{4,6},{6,4},{8,10},{10,8},{12,14},{14,12},{16,18},{18,... | collective-permute-start | bytes 737288 | tf_op jit(solution)/shard_map/ppermute | solution.py:354
  49.2 12.5 %collective-permute-start.9 = (f32[15,32,128]{2,1,0:T(8,128)S(1)}, f32[15,32,128]{2,1,0:T(8,128)S(1)}, u32[]{:S(2)}, u32[]{:S(2)}) collective-permute-start(f32[15,32,128]{2,1,0:T(8,128)S(1)} %get-tuple-element.131), channel_id=1, source_target_pairs={{2,4},{4,2},{6,8},{8,6},{10,12},{12,10},{14,16},{16,14},{18,20},{2... | collective-permute-start | bytes 737288 | tf_op jit(solution)/shard_map/ppermute | solution.py:354
  57.8 11.8 %collective-permute-start.13 = (f32[15,32,128]{2,1,0:T(8,128)S(1)}, f32[15,32,128]{2,1,0:T(8,128)S(1)}, u32[]{:S(2)}, u32[]{:S(2)}) collective-permute-start(f32[15,32,128]{2,1,0:T(8,128)S(1)} %get-tuple-element.140), channel_id=1, source_target_pairs={{2,4},{4,2},{6,8},{8,6},{10,12},{12,10},{14,16},{16,14},{18,20},{2... | collective-permute-start | bytes 737288 | tf_op jit(solution)/shard_map/ppermute | solution.py:354
  61.4 10.3 %collective-permute-start.16 = (f32[15,32,128]{2,1,0:T(8,128)S(1)}, f32[15,32,128]{2,1,0:T(8,128)S(1)}, u32[]{:S(2)}, u32[]{:S(2)}) collective-permute-start(f32[15,32,128]{2,1,0:T(8,128)S(1)} %get-tuple-element.142), channel_id=1, source_target_pairs={{0,2},{2,0},{4,6},{6,4},{8,10},{10,8},{12,14},{14,12},{16,18},{18,... | collective-permute-start | bytes 737288 | tf_op jit(solution)/shard_map/ppermute | solution.py:354
  61.7 11.5 %collective-permute-start.15 = (f32[16,32,128]{2,1,0:T(8,128)S(1)}, f32[16,32,128]{2,1,0:T(8,128)S(1)}, u32[]{:S(2)}, u32[]{:S(2)}) collective-permute-start(f32[16,32,128]{2,1,0:T(8,128)S(1)} %get-tuple-element.141.own.current), channel_id=1, source_target_pairs={{0,1},{1,0},{2,3},{3,2},{4,5},{5,4},{6,7},{7,6},{8,9},{9,8},{10,11... | collective-permute-start | bytes 786440 | tf_op jit(solution)/shard_map/ppermute | solution.py:358
  64.0 13.3 %collective-permute-start.18 = (f32[15,32,128]{2,1,0:T(8,128)S(1)}, f32[15,32,128]{2,1,0:T(8,128)S(1)}, u32[]{:S(2)}, u32[]{:S(2)}) collective-permute-start(f32[15,32,128]{2,1,0:T(8,128)S(1)} %get-tuple-element.148), channel_id=1, source_target_pairs={{2,4},{4,2},{6,8},{8,6},{10,12},{12,10},{14,16},{16,14},{18,20},{2... | collective-permute-start | bytes 737288 | tf_op jit(solution)/shard_map/ppermute | solution.py:354
  67.8 9.5 %collective-permute-start.19 = (f32[15,32,128]{2,1,0:T(8,128)S(1)}, f32[15,32,128]{2,1,0:T(8,128)S(1)}, u32[]{:S(2)}, u32[]{:S(2)}) collective-permute-start(f32[15,32,128]{2,1,0:T(8,128)S(1)} %get-tuple-element.149), channel_id=1, source_target_pairs={{0,2},{2,0},{4,6},{6,4},{8,10},{10,8},{12,14},{14,12},{16,18},{18,... | collective-permute-start | bytes 737288 | tf_op jit(solution)/shard_map/ppermute | solution.py:354
  69.6 3.6 %collective-permute-start.14 = (f32[15,32,128]{2,1,0:T(8,128)S(1)}, f32[15,32,128]{2,1,0:T(8,128)S(1)}, u32[]{:S(2)}, u32[]{:S(2)}) collective-permute-start(f32[15,32,128]{2,1,0:T(8,128)S(1)} %collective-permute-done.13.first), channel_id=1, source_target_pairs={{0,1},{1,0},{2,3},{3,2},{4,5},{5,4},{6,7},{7,6},{8,9},{9,8},{10,11... | collective-permute-start | bytes 737288 | tf_op jit(solution)/shard_map/ppermute | solution.py:358
  71.7 1.6 collective-permute-start.17
  84.1 12.2 %collective-permute-start.22 = (f32[15,32,128]{2,1,0:T(8,128)S(1)}, f32[15,32,128]{2,1,0:T(8,128)S(1)}, u32[]{:S(2)}, u32[]{:S(2)}) collective-permute-start(f32[15,32,128]{2,1,0:T(8,128)S(1)} %get-tuple-element.158), channel_id=1, source_target_pairs={{2,4},{4,2},{6,8},{8,6},{10,12},{12,10},{14,16},{16,14},{18,20},{2... | collective-permute-start | bytes 737288 | tf_op jit(solution)/shard_map/ppermute | solution.py:354
  87.8 8.6 %collective-permute-start.23 = (f32[15,32,128]{2,1,0:T(8,128)S(1)}, f32[15,32,128]{2,1,0:T(8,128)S(1)}, u32[]{:S(2)}, u32[]{:S(2)}) collective-permute-start(f32[15,32,128]{2,1,0:T(8,128)S(1)} %get-tuple-element.159), channel_id=1, source_target_pairs={{0,2},{2,0},{4,6},{6,4},{8,10},{10,8},{12,14},{14,12},{16,18},{18,... | collective-permute-start | bytes 737288 | tf_op jit(solution)/shard_map/ppermute | solution.py:354
  87.8 13.9 %collective-permute-start.20 = (f32[15,32,128]{2,1,0:T(8,128)S(1)}, f32[15,32,128]{2,1,0:T(8,128)S(1)}, u32[]{:S(2)}, u32[]{:S(2)}) collective-permute-start(f32[15,32,128]{2,1,0:T(8,128)S(1)} %get-tuple-element.155), channel_id=1, source_target_pairs={{2,4},{4,2},{6,8},{8,6},{10,12},{12,10},{14,16},{16,14},{18,20},{2... | collective-permute-start | bytes 737288 | tf_op jit(solution)/shard_map/ppermute | solution.py:354
  91.1 10.5 %collective-permute-start.21 = (f32[15,32,128]{2,1,0:T(8,128)S(1)}, f32[15,32,128]{2,1,0:T(8,128)S(1)}, u32[]{:S(2)}, u32[]{:S(2)}) collective-permute-start(f32[15,32,128]{2,1,0:T(8,128)S(1)} %get-tuple-element.156), channel_id=1, source_target_pairs={{0,2},{2,0},{4,6},{6,4},{8,10},{10,8},{12,14},{14,12},{16,18},{18,... | collective-permute-start | bytes 737288 | tf_op jit(solution)/shard_map/ppermute | solution.py:354
  97.1 11.1 %collective-permute-start.24 = (f32[15,32,128]{2,1,0:T(8,128)S(1)}, f32[15,32,128]{2,1,0:T(8,128)S(1)}, u32[]{:S(2)}, u32[]{:S(2)}) collective-permute-start(f32[15,32,128]{2,1,0:T(8,128)S(1)} %get-tuple-element.164), channel_id=1, source_target_pairs={{2,4},{4,2},{6,8},{8,6},{10,12},{12,10},{14,16},{16,14},{18,20},{2... | collective-permute-start | bytes 737288 | tf_op jit(solution)/shard_map/ppermute | solution.py:354
  100.7 11.0 %collective-permute-start.27 = (f32[15,32,128]{2,1,0:T(8,128)S(1)}, f32[15,32,128]{2,1,0:T(8,128)S(1)}, u32[]{:S(2)}, u32[]{:S(2)}) collective-permute-start(f32[15,32,128]{2,1,0:T(8,128)S(1)} %get-tuple-element.166), channel_id=1, source_target_pairs={{0,2},{2,0},{4,6},{6,4},{8,10},{10,8},{12,14},{14,12},{16,18},{18,... | collective-permute-start | bytes 737288 | tf_op jit(solution)/shard_map/ppermute | solution.py:354
  101.6 11.6 %collective-permute-start.26 = (f32[16,32,128]{2,1,0:T(8,128)S(1)}, f32[16,32,128]{2,1,0:T(8,128)S(1)}, u32[]{:S(2)}, u32[]{:S(2)}) collective-permute-start(f32[16,32,128]{2,1,0:T(8,128)S(1)} %get-tuple-element.165.own.current), channel_id=1, source_target_pairs={{0,1},{1,0},{2,3},{3,2},{4,5},{5,4},{6,7},{7,6},{8,9},{9,8},{10,11... | collective-permute-start | bytes 786440 | tf_op jit(solution)/shard_map/ppermute | solution.py:358
  104.7 13.1 %collective-permute-start.29 = (f32[15,32,128]{2,1,0:T(8,128)S(1)}, f32[15,32,128]{2,1,0:T(8,128)S(1)}, u32[]{:S(2)}, u32[]{:S(2)}) collective-permute-start(f32[15,32,128]{2,1,0:T(8,128)S(1)} %get-tuple-element.172), channel_id=1, source_target_pairs={{2,4},{4,2},{6,8},{8,6},{10,12},{12,10},{14,16},{16,14},{18,20},{2... | collective-permute-start | bytes 737288 | tf_op jit(solution)/shard_map/ppermute | solution.py:354
  108.1 9.6 %collective-permute-start.30 = (f32[15,32,128]{2,1,0:T(8,128)S(1)}, f32[15,32,128]{2,1,0:T(8,128)S(1)}, u32[]{:S(2)}, u32[]{:S(2)}) collective-permute-start(f32[15,32,128]{2,1,0:T(8,128)S(1)} %get-tuple-element.173), channel_id=1, source_target_pairs={{0,2},{2,0},{4,6},{6,4},{8,10},{10,8},{12,14},{14,12},{16,18},{18,... | collective-permute-start | bytes 737288 | tf_op jit(solution)/shard_map/ppermute | solution.py:354
  108.1 5.1 %collective-permute-start.25 = (f32[15,32,128]{2,1,0:T(8,128)S(1)}, f32[15,32,128]{2,1,0:T(8,128)S(1)}, u32[]{:S(2)}, u32[]{:S(2)}) collective-permute-start(f32[15,32,128]{2,1,0:T(8,128)S(1)} %collective-permute-done.24.first), channel_id=1, source_target_pairs={{0,1},{1,0},{2,3},{3,2},{4,5},{5,4},{6,7},{7,6},{8,9},{9,8},{10,11... | collective-permute-start | bytes 737288 | tf_op jit(solution)/shard_map/ppermute | solution.py:358
  111.7 1.6 collective-permute-start.28
  124.6 12.2 %collective-permute-start.33 = (f32[15,32,128]{2,1,0:T(8,128)S(1)}, f32[15,32,128]{2,1,0:T(8,128)S(1)}, u32[]{:S(2)}, u32[]{:S(2)}) collective-permute-start(f32[15,32,128]{2,1,0:T(8,128)S(1)} %get-tuple-element.182), channel_id=1, source_target_pairs={{2,4},{4,2},{6,8},{8,6},{10,12},{12,10},{14,16},{16,14},{18,20},{2... | collective-permute-start | bytes 737288 | tf_op jit(solution)/shard_map/ppermute | solution.py:354
  128.0 8.8 %collective-permute-start.34 = (f32[15,32,128]{2,1,0:T(8,128)S(1)}, f32[15,32,128]{2,1,0:T(8,128)S(1)}, u32[]{:S(2)}, u32[]{:S(2)}) collective-permute-start(f32[15,32,128]{2,1,0:T(8,128)S(1)} %get-tuple-element.183), channel_id=1, source_target_pairs={{0,2},{2,0},{4,6},{6,4},{8,10},{10,8},{12,14},{14,12},{16,18},{18,... | collective-permute-start | bytes 737288 | tf_op jit(solution)/shard_map/ppermute | solution.py:354
  128.0 14.0 %collective-permute-start.31 = (f32[15,32,128]{2,1,0:T(8,128)S(1)}, f32[15,32,128]{2,1,0:T(8,128)S(1)}, u32[]{:S(2)}, u32[]{:S(2)}) collective-permute-start(f32[15,32,128]{2,1,0:T(8,128)S(1)} %get-tuple-element.179), channel_id=1, source_target_pairs={{2,4},{4,2},{6,8},{8,6},{10,12},{12,10},{14,16},{16,14},{18,20},{2... | collective-permute-start | bytes 737288 | tf_op jit(solution)/shard_map/ppermute | solution.py:354
  131.6 10.5 %collective-permute-start.32 = (f32[15,32,128]{2,1,0:T(8,128)S(1)}, f32[15,32,128]{2,1,0:T(8,128)S(1)}, u32[]{:S(2)}, u32[]{:S(2)}) collective-permute-start(f32[15,32,128]{2,1,0:T(8,128)S(1)} %get-tuple-element.180), channel_id=1, source_target_pairs={{0,2},{2,0},{4,6},{6,4},{8,10},{10,8},{12,14},{14,12},{16,18},{18,... | collective-permute-start | bytes 737288 | tf_op jit(solution)/shard_map/ppermute | solution.py:354
  137.5 11.1 %collective-permute-start.35 = (f32[15,32,128]{2,1,0:T(8,128)S(1)}, f32[15,32,128]{2,1,0:T(8,128)S(1)}, u32[]{:S(2)}, u32[]{:S(2)}) collective-permute-start(f32[15,32,128]{2,1,0:T(8,128)S(1)} %get-tuple-element.188), channel_id=1, source_target_pairs={{2,4},{4,2},{6,8},{8,6},{10,12},{12,10},{14,16},{16,14},{18,20},{2... | collective-permute-start | bytes 737288 | tf_op jit(solution)/shard_map/ppermute | solution.py:354
  140.9 11.3 %collective-permute-start.38 = (f32[15,32,128]{2,1,0:T(8,128)S(1)}, f32[15,32,128]{2,1,0:T(8,128)S(1)}, u32[]{:S(2)}, u32[]{:S(2)}) collective-permute-start(f32[15,32,128]{2,1,0:T(8,128)S(1)} %get-tuple-element.190), channel_id=1, source_target_pairs={{0,2},{2,0},{4,6},{6,4},{8,10},{10,8},{12,14},{14,12},{16,18},{18,... | collective-permute-start | bytes 737288 | tf_op jit(solution)/shard_map/ppermute | solution.py:354
  142.0 11.7 %collective-permute-start.37 = (f32[16,32,128]{2,1,0:T(8,128)S(1)}, f32[16,32,128]{2,1,0:T(8,128)S(1)}, u32[]{:S(2)}, u32[]{:S(2)}) collective-permute-start(f32[16,32,128]{2,1,0:T(8,128)S(1)} %get-tuple-element.189.own.current), channel_id=1, source_target_pairs={{0,1},{1,0},{2,3},{3,2},{4,5},{5,4},{6,7},{7,6},{8,9},{9,8},{10,11... | collective-permute-start | bytes 786440 | tf_op jit(solution)/shard_map/ppermute | solution.py:358
  145.0 13.1 %collective-permute-start.40 = (f32[15,32,128]{2,1,0:T(8,128)S(1)}, f32[15,32,128]{2,1,0:T(8,128)S(1)}, u32[]{:S(2)}, u32[]{:S(2)}) collective-permute-start(f32[15,32,128]{2,1,0:T(8,128)S(1)} %get-tuple-element.196), channel_id=1, source_target_pairs={{2,4},{4,2},{6,8},{8,6},{10,12},{12,10},{14,16},{16,14},{18,20},{2... | collective-permute-start | bytes 737288 | tf_op jit(solution)/shard_map/ppermute | solution.py:354
  148.6 9.5 %collective-permute-start.41 = (f32[15,32,128]{2,1,0:T(8,128)S(1)}, f32[15,32,128]{2,1,0:T(8,128)S(1)}, u32[]{:S(2)}, u32[]{:S(2)}) collective-permute-start(f32[15,32,128]{2,1,0:T(8,128)S(1)} %get-tuple-element.197), channel_id=1, source_target_pairs={{0,2},{2,0},{4,6},{6,4},{8,10},{10,8},{12,14},{14,12},{16,18},{18,... | collective-permute-start | bytes 737288 | tf_op jit(solution)/shard_map/ppermute | solution.py:354
  148.6 5.1 %collective-permute-start.36 = (f32[15,32,128]{2,1,0:T(8,128)S(1)}, f32[15,32,128]{2,1,0:T(8,128)S(1)}, u32[]{:S(2)}, u32[]{:S(2)}) collective-permute-start(f32[15,32,128]{2,1,0:T(8,128)S(1)} %collective-permute-done.35.first), channel_id=1, source_target_pairs={{0,1},{1,0},{2,3},{3,2},{4,5},{5,4},{6,7},{7,6},{8,9},{9,8},{10,11... | collective-permute-start | bytes 737288 | tf_op jit(solution)/shard_map/ppermute | solution.py:358
  152.2 1.6 collective-permute-start.39
  164.9 12.2 %collective-permute-start.44 = (f32[15,32,128]{2,1,0:T(8,128)S(1)}, f32[15,32,128]{2,1,0:T(8,128)S(1)}, u32[]{:S(2)}, u32[]{:S(2)}) collective-permute-start(f32[15,32,128]{2,1,0:T(8,128)S(1)} %get-tuple-element.206), channel_id=1, source_target_pairs={{2,4},{4,2},{6,8},{8,6},{10,12},{12,10},{14,16},{16,14},{18,20},{2... | collective-permute-start | bytes 737288 | tf_op jit(solution)/shard_map/ppermute | solution.py:354
  168.5 8.6 %collective-permute-start.45 = (f32[15,32,128]{2,1,0:T(8,128)S(1)}, f32[15,32,128]{2,1,0:T(8,128)S(1)}, u32[]{:S(2)}, u32[]{:S(2)}) collective-permute-start(f32[15,32,128]{2,1,0:T(8,128)S(1)} %get-tuple-element.207), channel_id=1, source_target_pairs={{0,2},{2,0},{4,6},{6,4},{8,10},{10,8},{12,14},{14,12},{16,18},{18,... | collective-permute-start | bytes 737288 | tf_op jit(solution)/shard_map/ppermute | solution.py:354
  168.5 13.8 %collective-permute-start.42 = (f32[15,32,128]{2,1,0:T(8,128)S(1)}, f32[15,32,128]{2,1,0:T(8,128)S(1)}, u32[]{:S(2)}, u32[]{:S(2)}) collective-permute-start(f32[15,32,128]{2,1,0:T(8,128)S(1)} %get-tuple-element.203), channel_id=1, source_target_pairs={{2,4},{4,2},{6,8},{8,6},{10,12},{12,10},{14,16},{16,14},{18,20},{2... | collective-permute-start | bytes 737288 | tf_op jit(solution)/shard_map/ppermute | solution.py:354
  171.9 10.5 %collective-permute-start.43 = (f32[15,32,128]{2,1,0:T(8,128)S(1)}, f32[15,32,128]{2,1,0:T(8,128)S(1)}, u32[]{:S(2)}, u32[]{:S(2)}) collective-permute-start(f32[15,32,128]{2,1,0:T(8,128)S(1)} %get-tuple-element.204), channel_id=1, source_target_pairs={{0,2},{2,0},{4,6},{6,4},{8,10},{10,8},{12,14},{14,12},{16,18},{18,... | collective-permute-start | bytes 737288 | tf_op jit(solution)/shard_map/ppermute | solution.py:354
  182.3 2.9 %collective-permute-start.47 = (f32[16,32,128]{2,1,0:T(8,128)S(1)}, f32[16,32,128]{2,1,0:T(8,128)S(1)}, u32[]{:S(2)}, u32[]{:S(2)}) collective-permute-start(f32[16,32,128]{2,1,0:T(8,128)S(1)} %update.14), channel_id=1, source_target_pairs={{0,1},{1,0},{2,3},{3,2},{4,5},{5,4},{6,7},{7,6},{8,9},{9,8},{10,11... | collective-permute-start | bytes 786440 | tf_op jit(solution)/shard_map/ppermute | solution.py:358
  184.7 1.6 collective-permute-start.46
  (12 other events, 60.8 us)
where the time goes:
time: 188 us; the launch traced here: 187 us
  starting transfers between devices  86.6 us (46%)
  Pallas kernels  54.4 us (29%)
  waiting for transfers between devices  38.6 us (21%)
  local copies, waits for them, and re-layouts  4.19 us (2%)
  other arithmetic  3.1 us (2%)
    ppermute x30, starting transfers between devices, exchange(): return lax.ppermute(x, 'tile', pairs)  59.4 us
    ppermute x30, waiting for transfers between devices, exchange(): return lax.ppermute(x, 'tile', pairs)  37.1 us
    pallas_call x4, Pallas kernels, correct(): pl.pallas_call(correct_kernel, out_shape=[jax.ShapeDtypeStruct(s, F32) fo...  21.8 us
    ppermute x16, starting transfers between devices, swap(): return lax.ppermute(x, 'view', [(0, 1), (1, 0)])  20.3 us
    pallas_call x12, Pallas kernels, blur(): pl.pallas_call(functools.partial(blur_kernel, at), out_shape=[jax.ShapeDt...  18.3 us
    pallas_call x8, Pallas kernels, update(): pl.pallas_call(add_neighbours if last else update_kernel, out_shape=[jax....  5.52 us
    ppermute x1, starting transfers between devices, per_device(): after = lax.ppermute(cover, 'tile', [(j, i) for i, j in ring])  5.15 us
    pallas_call x1, Pallas kernels, make_matrices(): pl.pallas_call(matrices_kernel, out_shape=[jax.ShapeDtypeStruct(s, BF16)...  4.82 us
  transfers between devices with their start and end apart: 48, of which 14 were waited for; matrix products, arithmetic and copies ran while one was open for 0% of the time, Pallas kernels for 14%

commit v1 on v0

--- a/solution.py
+++ b/solution.py
@@ -213,7 +213,7 @@
         out_shape=[jax.ShapeDtypeStruct((VIEWS * W, PART, NZ), BF16)] * 2,
         in_specs=[VMEM] * 5,
         out_specs=[VMEM] * 2,
-        scratch_shapes=[pltpu.VMEM((SLOTS * PART_STEP, NZ), F32), pltpu.VMEM((VIEWS * W * PART_STEP, NZ), F32)],
+        scratch_shapes=[pltpu.VMEM(((SLOTS + 8) * PART_STEP, NZ), F32), pltpu.VMEM(((VIEWS * W + 8) * PART_STEP, NZ), F32)],
         compiler_params=pltpu.CompilerParams(vmem_limit_bytes=10 << 20),
         cost_estimate=pl.CostEstimate(flops=10_000_000_000, bytes_accessed=3_000_000, transcendentals=0),
         name="blur",
@@ -263,8 +263,8 @@
         in_specs=[VMEM] * 12,
         out_specs=[VMEM] * 6,
         scratch_shapes=[
-            pltpu.VMEM((VIEWS * W * OWN_STEP, NZ), F32),
-            pltpu.VMEM((SLOTS * OWN_STEP, NZ), F32),
+            pltpu.VMEM(((VIEWS * W + 8) * OWN_STEP, NZ), F32),
+            pltpu.VMEM(((SLOTS + 8) * OWN_STEP, NZ), F32),
         ],
         compiler_params=pltpu.CompilerParams(vmem_limit_bytes=26 << 20),
         cost_estimate=pl.CostEstimate(flops=4_000_000_000, bytes_accessed=16_000_000, transcendentals=0),

time: 188 us -> 188 us (level)
  no operation moved by 1% of the time
where the time goes in v1:
time: 188 us; the launch traced here: 187 us
  starting transfers between devices  86.6 us (46%)
  Pallas kernels  54.4 us (29%)
  waiting for transfers between devices  38.6 us (21%)
  local copies, waits for them, and re-layouts  4.19 us (2%)
  other arithmetic  3.1 us (2%)
    ppermute x30, starting transfers between devices, exchange(): return lax.ppermute(x, 'tile', pairs)  59.4 us
    ppermute x30, waiting for transfers between devices, exchange(): return lax.ppermute(x, 'tile', pairs)  37.1 us
    pallas_call x4, Pallas kernels, correct(): pl.pallas_call(correct_kernel, out_shape=[jax.ShapeDtypeStruct(s, F32) fo...  21.8 us
    ppermute x16, starting transfers between devices, swap(): return lax.ppermute(x, 'view', [(0, 1), (1, 0)])  20.4 us
    pallas_call x12, Pallas kernels, blur(): pl.pallas_call(functools.partial(blur_kernel, at), out_shape=[jax.ShapeDt...  18.3 us
    pallas_call x8, Pallas kernels, update(): pl.pallas_call(add_neighbours if last else update_kernel, out_shape=[jax....  5.52 us
    ppermute x1, starting transfers between devices, per_device(): after = lax.ppermute(cover, 'tile', [(j, i) for i, j in ring])  5.15 us
    pallas_call x1, Pallas kernels, make_matrices(): pl.pallas_call(matrices_kernel, out_shape=[jax.ShapeDtypeStruct(s, BF16)...  4.82 us
  transfers between devices with their start and end apart: 48, of which 14 were waited for; matrix products, arithmetic and copies ran while one was open for 0% of the time, Pallas kernels for 14%

profile of v1, /device:TPU:1, one launch (start us, length us, event | category | flops | bytes accessed | tf_op | source)
XLA Modules:
  0.0 187.4 jit_solution(13236086264690848243)
XLA Ops:
  1.3 1.6 begin.1
  6.1 8.5 %collective-permute-start.1 = (f32[15,64,128]{2,1,0:T(8,128)}, f32[15,64,128]{2,1,0:T(8,128)S(1)}, u32[]{:S(2)}, u32[]{:S(2)}) collective-permute-start(f32[15,64,128]{2,1,0:T(8,128)} %get-tuple-element.114), channel_id=1, source_target_pairs={{2,4},{4,2},{6,8},{8,6},{10,12},{12,10},{14,16},{16,14},{18,20},{2... | collective-permute-start | bytes 1474568 | tf_op jit(solution)/shard_map/ppermute | solution.py:354
  15.1 1.7 collective-permute-start.7
  16.9 5.2 %collective-permute-start.8 = (f32[96]{0:T(128)S(1)}, f32[96]{0:T(128)S(1)}, u32[]{:S(2)}, u32[]{:S(2)}) collective-permute-start(f32[96]{0:T(128)S(1)} %pad_maximum_fusion.4), channel_id=1, source_target_pairs={{2,0},{4,2},{6,4},{8,6},{10,8},{12,10},{14,12},{16,14},{18,16},{20... | collective-permute-start | bytes 1160 | tf_op jit(solution)/shard_map/ppermute | solution.py:378
  22.1 4.8 %matrices.1 = (bf16[192,96]{1,0:T(8,128)(2,1)S(1)}, bf16[6,160,192]{2,1,0:T(8,128)(2,1)S(1)}, bf16[6,128,160]{2,1,0:T(8,128)(2,1)S(1)}, bf16[6,256,256]{2,1,0:T(8,128)(2,1)S(1)}, bf16[6,256,256]{2,1,0:T(8,128)(2,1)S(1)}) custom-call(s32[3]{0:T(128)S(1)} %pad_add_fusion.where, f32[558]{0:T(1024)S(1)} %pad_maximum_fusion.1.taps), custom_call_target="tpu_custom_call" | custom-call | flops 1000 | bytes 1000 | tf_op jit(solution)/shard_map/matrices/pallas_call | solution.py:120
  27.0 1.9 %copy-done = f32[3,16,128,128]{3,2,1,0:T(8,128)S(1)} copy-done((f32[3,16,128,128]{3,2,1,0:T(8,128)S(1)}, f32[3,16,128,128]{3,2,1,0:T(8,128)}, u32[]{:S(2)}) %copy-start) | copy-done | bytes 3145752
  30.5 1.6 cover_matrix.1.xt
  35.8 1.5 blur.14
  37.4 6.0 %correct.4 = (f32[15,32,128]{2,1,0:T(8,128)}, f32[16,32,128]{2,1,0:T(8,128)S(1)}, f32[15,32,128]{2,1,0:T(8,128)}, f32[15,32,128]{2,1,0:T(8,128)S(1)}, f32[16,32,...) custom-call(bf16[96,32,128]{2,1,0:T(8,128)(2,1)S(1)} %get-tuple-element.118.near_high, ...), custom_call_target="tpu_custom_call" | custom-call | flops 4000000000 | bytes 16000000 | tf_op jit(solution)/shard_map/correct/pallas_call | solution.py:260
  44.0 3.5 %collective-permute-start.11 = (f32[15,32,128]{2,1,0:T(8,128)}, f32[15,32,128]{2,1,0:T(8,128)S(1)}, u32[]{:S(2)}, u32[]{:S(2)}) collective-permute-start(f32[15,32,128]{2,1,0:T(8,128)} %get-tuple-element.134), channel_id=1, source_target_pairs={{2,4},{4,2},{6,8},{8,6},{10,12},{12,10},{14,16},{16,14},{18,20},{2... | collective-permute-start | bytes 737288 | tf_op jit(solution)/shard_map/ppermute | solution.py:354
  47.7 1.5 collective-permute-start.10
  49.2 3.4 %collective-permute-start.9 = (f32[15,32,128]{2,1,0:T(8,128)S(1)}, f32[15,32,128]{2,1,0:T(8,128)S(1)}, u32[]{:S(2)}, u32[]{:S(2)}) collective-permute-start(f32[15,32,128]{2,1,0:T(8,128)S(1)} %get-tuple-element.131), channel_id=1, source_target_pairs={{2,4},{4,2},{6,8},{8,6},{10,12},{12,10},{14,16},{16,14},{18,20},{2... | collective-permute-start | bytes 737288 | tf_op jit(solution)/shard_map/ppermute | solution.py:354
  52.6 4.5 %collective-permute-done.11.from1 = f32[15,32,128]{2,1,0:T(8,128)S(1)} collective-permute-done((f32[15,32,128]{2,1,0:T(8,128)}, f32[15,32,128]{2,1,0:T(8,128)S(1)}, u32[]{:S(2)}, u32[]{:S(2)}) %collective-permute-start.11) | collective-permute-done | bytes 245792 | tf_op jit(solution)/shard_map/ppermute | solution.py:354
  57.8 3.6 %collective-permute-start.13 = (f32[15,32,128]{2,1,0:T(8,128)S(1)}, f32[15,32,128]{2,1,0:T(8,128)S(1)}, u32[]{:S(2)}, u32[]{:S(2)}) collective-permute-start(f32[15,32,128]{2,1,0:T(8,128)S(1)} %get-tuple-element.140), channel_id=1, source_target_pairs={{2,4},{4,2},{6,8},{8,6},{10,12},{12,10},{14,16},{16,14},{18,20},{2... | collective-permute-start | bytes 737288 | tf_op jit(solution)/shard_map/ppermute | solution.py:354
  61.7 1.6 collective-permute-start.15
  64.0 3.8 %collective-permute-start.18 = (f32[15,32,128]{2,1,0:T(8,128)S(1)}, f32[15,32,128]{2,1,0:T(8,128)S(1)}, u32[]{:S(2)}, u32[]{:S(2)}) collective-permute-start(f32[15,32,128]{2,1,0:T(8,128)S(1)} %get-tuple-element.148), channel_id=1, source_target_pairs={{2,4},{4,2},{6,8},{8,6},{10,12},{12,10},{14,16},{16,14},{18,20},{2... | collective-permute-start | bytes 737288 | tf_op jit(solution)/shard_map/ppermute | solution.py:354
  67.8 1.8 collective-permute-done.13.first
  69.6 2.1 %collective-permute-start.14 = (f32[15,32,128]{2,1,0:T(8,128)S(1)}, f32[15,32,128]{2,1,0:T(8,128)S(1)}, u32[]{:S(2)}, u32[]{:S(2)}) collective-permute-start(f32[15,32,128]{2,1,0:T(8,128)S(1)} %collective-permute-done.13.first), channel_id=1, source_target_pairs={{0,1},{1,0},{2,3},{3,2},{4,5},{5,4},{6,7},{7,6},{8,9},{9,8},{10,11... | collective-permute-start | bytes 737288 | tf_op jit(solution)/shard_map/ppermute | solution.py:358
  71.7 1.5 blur.16
  73.3 1.5 blur.15
  74.8 2.5 %collective-permute-done.18.first = f32[15,32,128]{2,1,0:T(8,128)S(1)} collective-permute-done((f32[15,32,128]{2,1,0:T(8,128)S(1)}, f32[15,32,128]{2,1,0:T(8,128)S(1)}, u32[]{:S(2)}, u32[]{:S(2)}) %collective-permute-start.18) | collective-permute-done | bytes 245792 | tf_op jit(solution)/shard_map/ppermute | solution.py:354
  77.3 1.5 blur.17
  78.9 5.3 %correct.5 = (f32[15,32,128]{2,1,0:T(8,128)S(1)}, f32[16,32,128]{2,1,0:T(8,128)S(1)}, f32[15,32,128]{2,1,0:T(8,128)S(1)}, f32[15,32,128]{2,1,0:T(8,128)S(1)}, f3...) custom-call(bf16[96,32,128]{2,1,0:T(8,128)(2,1)S(1)} %get-tuple-element.146.near_high, ...), custom_call_target="tpu_custom_call" | custom-call | flops 4000000000 | bytes 16000000 | tf_op jit(solution)/shard_map/correct/pallas_call | solution.py:260
  84.2 3.6 %collective-permute-start.22 = (f32[15,32,128]{2,1,0:T(8,128)S(1)}, f32[15,32,128]{2,1,0:T(8,128)S(1)}, u32[]{:S(2)}, u32[]{:S(2)}) collective-permute-start(f32[15,32,128]{2,1,0:T(8,128)S(1)} %get-tuple-element.158), channel_id=1, source_target_pairs={{2,4},{4,2},{6,8},{8,6},{10,12},{12,10},{14,16},{16,14},{18,20},{2... | collective-permute-start | bytes 737288 | tf_op jit(solution)/shard_map/ppermute | solution.py:354
  87.8 3.4 %collective-permute-start.20 = (f32[15,32,128]{2,1,0:T(8,128)S(1)}, f32[15,32,128]{2,1,0:T(8,128)S(1)}, u32[]{:S(2)}, u32[]{:S(2)}) collective-permute-start(f32[15,32,128]{2,1,0:T(8,128)S(1)} %get-tuple-element.155), channel_id=1, source_target_pairs={{2,4},{4,2},{6,8},{8,6},{10,12},{12,10},{14,16},{16,14},{18,20},{2... | collective-permute-start | bytes 737288 | tf_op jit(solution)/shard_map/ppermute | solution.py:354
  91.2 5.2 %collective-permute-done.22.from1 = f32[15,32,128]{2,1,0:T(8,128)S(1)} collective-permute-done((f32[15,32,128]{2,1,0:T(8,128)S(1)}, f32[15,32,128]{2,1,0:T(8,128)S(1)}, u32[]{:S(2)}, u32[]{:S(2)}) %collective-permute-start.22) | collective-permute-done | bytes 245792 | tf_op jit(solution)/shard_map/ppermute | solution.py:354
  97.1 3.6 %collective-permute-start.24 = (f32[15,32,128]{2,1,0:T(8,128)S(1)}, f32[15,32,128]{2,1,0:T(8,128)S(1)}, u32[]{:S(2)}, u32[]{:S(2)}) collective-permute-start(f32[15,32,128]{2,1,0:T(8,128)S(1)} %get-tuple-element.164), channel_id=1, source_target_pairs={{2,4},{4,2},{6,8},{8,6},{10,12},{12,10},{14,16},{16,14},{18,20},{2... | collective-permute-start | bytes 737288 | tf_op jit(solution)/shard_map/ppermute | solution.py:354
  101.7 2.4 %collective-permute-start.26 = (f32[16,32,128]{2,1,0:T(8,128)S(1)}, f32[16,32,128]{2,1,0:T(8,128)S(1)}, u32[]{:S(2)}, u32[]{:S(2)}) collective-permute-start(f32[16,32,128]{2,1,0:T(8,128)S(1)} %get-tuple-element.165.own.current), channel_id=1, source_target_pairs={{0,1},{1,0},{2,3},{3,2},{4,5},{5,4},{6,7},{7,6},{8,9},{9,8},{10,11... | collective-permute-start | bytes 786440 | tf_op jit(solution)/shard_map/ppermute | solution.py:358
  104.7 3.4 %collective-permute-start.29 = (f32[15,32,128]{2,1,0:T(8,128)S(1)}, f32[15,32,128]{2,1,0:T(8,128)S(1)}, u32[]{:S(2)}, u32[]{:S(2)}) collective-permute-start(f32[15,32,128]{2,1,0:T(8,128)S(1)} %get-tuple-element.172), channel_id=1, source_target_pairs={{2,4},{4,2},{6,8},{8,6},{10,12},{12,10},{14,16},{16,14},{18,20},{2... | collective-permute-start | bytes 737288 | tf_op jit(solution)/shard_map/ppermute | solution.py:354
  108.2 3.6 %collective-permute-start.25 = (f32[15,32,128]{2,1,0:T(8,128)S(1)}, f32[15,32,128]{2,1,0:T(8,128)S(1)}, u32[]{:S(2)}, u32[]{:S(2)}) collective-permute-start(f32[15,32,128]{2,1,0:T(8,128)S(1)} %collective-permute-done.24.first), channel_id=1, source_target_pairs={{0,1},{1,0},{2,3},{3,2},{4,5},{5,4},{6,7},{7,6},{8,9},{9,8},{10,11... | collective-permute-start | bytes 737288 | tf_op jit(solution)/shard_map/ppermute | solution.py:358
  113.3 1.5 blur.18
  114.8 2.9 %collective-permute-done.29.first = f32[15,32,128]{2,1,0:T(8,128)S(1)} collective-permute-done((f32[15,32,128]{2,1,0:T(8,128)S(1)}, f32[15,32,128]{2,1,0:T(8,128)S(1)}, u32[]{:S(2)}, u32[]{:S(2)}) %collective-permute-start.29) | collective-permute-done | bytes 245792 | tf_op jit(solution)/shard_map/ppermute | solution.py:354
  117.8 1.5 blur.20
  119.3 5.3 %correct.6 = (f32[15,32,128]{2,1,0:T(8,128)S(1)}, f32[16,32,128]{2,1,0:T(8,128)S(1)}, f32[15,32,128]{2,1,0:T(8,128)S(1)}, f32[15,32,128]{2,1,0:T(8,128)S(1)}, f3...) custom-call(bf16[96,32,128]{2,1,0:T(8,128)(2,1)S(1)} %get-tuple-element.170.near_high, ...), custom_call_target="tpu_custom_call" | custom-call | flops 4000000000 | bytes 16000000 | tf_op jit(solution)/shard_map/correct/pallas_call | solution.py:260
  124.6 3.4 %collective-permute-start.33 = (f32[15,32,128]{2,1,0:T(8,128)S(1)}, f32[15,32,128]{2,1,0:T(8,128)S(1)}, u32[]{:S(2)}, u32[]{:S(2)}) collective-permute-start(f32[15,32,128]{2,1,0:T(8,128)S(1)} %get-tuple-element.182), channel_id=1, source_target_pairs={{2,4},{4,2},{6,8},{8,6},{10,12},{12,10},{14,16},{16,14},{18,20},{2... | collective-permute-start | bytes 737288 | tf_op jit(solution)/shard_map/ppermute | solution.py:354
  128.1 3.5 %collective-permute-start.31 = (f32[15,32,128]{2,1,0:T(8,128)S(1)}, f32[15,32,128]{2,1,0:T(8,128)S(1)}, u32[]{:S(2)}, u32[]{:S(2)}) collective-permute-start(f32[15,32,128]{2,1,0:T(8,128)S(1)} %get-tuple-element.179), channel_id=1, source_target_pairs={{2,4},{4,2},{6,8},{8,6},{10,12},{12,10},{14,16},{16,14},{18,20},{2... | collective-permute-start | bytes 737288 | tf_op jit(solution)/shard_map/ppermute | solution.py:354
  131.6 5.2 %collective-permute-done.33.from1 = f32[15,32,128]{2,1,0:T(8,128)S(1)} collective-permute-done((f32[15,32,128]{2,1,0:T(8,128)S(1)}, f32[15,32,128]{2,1,0:T(8,128)S(1)}, u32[]{:S(2)}, u32[]{:S(2)}) %collective-permute-start.33) | collective-permute-done | bytes 245792 | tf_op jit(solution)/shard_map/ppermute | solution.py:354
  137.5 3.4 %collective-permute-start.35 = (f32[15,32,128]{2,1,0:T(8,128)S(1)}, f32[15,32,128]{2,1,0:T(8,128)S(1)}, u32[]{:S(2)}, u32[]{:S(2)}) collective-permute-start(f32[15,32,128]{2,1,0:T(8,128)S(1)} %get-tuple-element.188), channel_id=1, source_target_pairs={{2,4},{4,2},{6,8},{8,6},{10,12},{12,10},{14,16},{16,14},{18,20},{2... | collective-permute-start | bytes 737288 | tf_op jit(solution)/shard_map/ppermute | solution.py:354
  142.1 2.2 %collective-permute-start.37 = (f32[16,32,128]{2,1,0:T(8,128)S(1)}, f32[16,32,128]{2,1,0:T(8,128)S(1)}, u32[]{:S(2)}, u32[]{:S(2)}) collective-permute-start(f32[16,32,128]{2,1,0:T(8,128)S(1)} %get-tuple-element.189.own.current), channel_id=1, source_target_pairs={{0,1},{1,0},{2,3},{3,2},{4,5},{5,4},{6,7},{7,6},{8,9},{9,8},{10,11... | collective-permute-start | bytes 786440 | tf_op jit(solution)/shard_map/ppermute | solution.py:358
  145.0 3.6 %collective-permute-start.40 = (f32[15,32,128]{2,1,0:T(8,128)S(1)}, f32[15,32,128]{2,1,0:T(8,128)S(1)}, u32[]{:S(2)}, u32[]{:S(2)}) collective-permute-start(f32[15,32,128]{2,1,0:T(8,128)S(1)} %get-tuple-element.196), channel_id=1, source_target_pairs={{2,4},{4,2},{6,8},{8,6},{10,12},{12,10},{14,16},{16,14},{18,20},{2... | collective-permute-start | bytes 737288 | tf_op jit(solution)/shard_map/ppermute | solution.py:354
  148.6 3.6 %collective-permute-start.36 = (f32[15,32,128]{2,1,0:T(8,128)S(1)}, f32[15,32,128]{2,1,0:T(8,128)S(1)}, u32[]{:S(2)}, u32[]{:S(2)}) collective-permute-start(f32[15,32,128]{2,1,0:T(8,128)S(1)} %collective-permute-done.35.first), channel_id=1, source_target_pairs={{0,1},{1,0},{2,3},{3,2},{4,5},{5,4},{6,7},{7,6},{8,9},{9,8},{10,11... | collective-permute-start | bytes 737288 | tf_op jit(solution)/shard_map/ppermute | solution.py:358
  155.3 2.8 %collective-permute-done.40.first = f32[15,32,128]{2,1,0:T(8,128)S(1)} collective-permute-done((f32[15,32,128]{2,1,0:T(8,128)S(1)}, f32[15,32,128]{2,1,0:T(8,128)S(1)}, u32[]{:S(2)}, u32[]{:S(2)}) %collective-permute-start.40) | collective-permute-done | bytes 245792 | tf_op jit(solution)/shard_map/ppermute | solution.py:354
  159.6 5.3 %correct.7 = (f32[15,32,128]{2,1,0:T(8,128)S(1)}, f32[16,32,128]{2,1,0:T(8,128)S(1)}, f32[15,32,128]{2,1,0:T(8,128)S(1)}, f32[15,32,128]{2,1,0:T(8,128)S(1)}, f3...) custom-call(bf16[96,32,128]{2,1,0:T(8,128)(2,1)S(1)} %get-tuple-element.194.near_high, ...), custom_call_target="tpu_custom_call" | custom-call | flops 4000000000 | bytes 16000000 | tf_op jit(solution)/shard_map/correct/pallas_call | solution.py:260
  164.9 3.6 %collective-permute-start.44 = (f32[15,32,128]{2,1,0:T(8,128)S(1)}, f32[15,32,128]{2,1,0:T(8,128)S(1)}, u32[]{:S(2)}, u32[]{:S(2)}) collective-permute-start(f32[15,32,128]{2,1,0:T(8,128)S(1)} %get-tuple-element.206), channel_id=1, source_target_pairs={{2,4},{4,2},{6,8},{8,6},{10,12},{12,10},{14,16},{16,14},{18,20},{2... | collective-permute-start | bytes 737288 | tf_op jit(solution)/shard_map/ppermute | solution.py:354
  168.5 3.4 %collective-permute-start.42 = (f32[15,32,128]{2,1,0:T(8,128)S(1)}, f32[15,32,128]{2,1,0:T(8,128)S(1)}, u32[]{:S(2)}, u32[]{:S(2)}) collective-permute-start(f32[15,32,128]{2,1,0:T(8,128)S(1)} %get-tuple-element.203), channel_id=1, source_target_pairs={{2,4},{4,2},{6,8},{8,6},{10,12},{12,10},{14,16},{16,14},{18,20},{2... | collective-permute-start | bytes 737288 | tf_op jit(solution)/shard_map/ppermute | solution.py:354
  171.9 5.2 %collective-permute-done.44.from1 = f32[15,32,128]{2,1,0:T(8,128)S(1)} collective-permute-done((f32[15,32,128]{2,1,0:T(8,128)S(1)}, f32[15,32,128]{2,1,0:T(8,128)S(1)}, u32[]{:S(2)}, u32[]{:S(2)}) %collective-permute-start.44) | collective-permute-done | bytes 245792 | tf_op jit(solution)/shard_map/ppermute | solution.py:354
  177.8 4.6 %collective-permute-done.42.from1 = f32[15,32,128]{2,1,0:T(8,128)S(1)} collective-permute-done((f32[15,32,128]{2,1,0:T(8,128)S(1)}, f32[15,32,128]{2,1,0:T(8,128)S(1)}, u32[]{:S(2)}, u32[]{:S(2)}) %collective-permute-start.42) | collective-permute-done | bytes 245792 | tf_op jit(solution)/shard_map/ppermute | solution.py:354
  182.4 1.7 collective-permute-start.47
  (118 shorter events, 28.1 us)
Async XLA Ops:
  4.7 10.3 %collective-permute-start = (f32[327]{0:T(512)S(1)}, f32[327]{0:T(512)S(1)}, u32[]{:S(2)}, u32[]{:S(2)}) collective-permute-start(f32[327]{0:T(512)S(1)} %pad_maximum_fusion.2), channel_id=1, source_target_pairs={{0,1},{1,0},{2,3},{3,2},{4,5},{5,4},{6,7},{7,6},{8,9},{9,8},{10,11... | collective-permute-start | bytes 3932 | tf_op jit(solution)/shard_map/ppermute | solution.py:358
  6.1 26.0 %collective-permute-start.1 = (f32[15,64,128]{2,1,0:T(8,128)}, f32[15,64,128]{2,1,0:T(8,128)S(1)}, u32[]{:S(2)}, u32[]{:S(2)}) collective-permute-start(f32[15,64,128]{2,1,0:T(8,128)} %get-tuple-element.114), channel_id=1, source_target_pairs={{2,4},{4,2},{6,8},{8,6},{10,12},{12,10},{14,16},{16,14},{18,20},{2... | collective-permute-start | bytes 1474568 | tf_op jit(solution)/shard_map/ppermute | solution.py:354
  14.6 17.6 %collective-permute-start.2 = (f32[15,64,128]{2,1,0:T(8,128)}, f32[15,64,128]{2,1,0:T(8,128)S(1)}, u32[]{:S(2)}, u32[]{:S(2)}) collective-permute-start(f32[15,64,128]{2,1,0:T(8,128)} %get-tuple-element.115), channel_id=1, source_target_pairs={{0,2},{2,0},{4,6},{6,4},{8,10},{10,8},{12,14},{14,12},{16,18},{18,... | collective-permute-start | bytes 1474568 | tf_op jit(solution)/shard_map/ppermute | solution.py:354
  14.6 21.1 %collective-permute-start.4 = (f32[16,64,128]{2,1,0:T(8,128)S(1)}, f32[16,64,128]{2,1,0:T(8,128)S(1)}, u32[]{:S(2)}, u32[]{:S(2)}) collective-permute-start(f32[16,64,128]{2,1,0:T(8,128)S(1)} %get-tuple-element.113.own), channel_id=1, source_target_pairs={{0,1},{1,0},{2,3},{3,2},{4,5},{5,4},{6,7},{7,6},{8,9},{9,8},{10,11... | collective-permute-start | bytes 1572872 | tf_op jit(solution)/shard_map/ppermute | solution.py:358
  15.1 14.6 %collective-permute-start.7 = (f32[96]{0:T(128)S(1)}, f32[96]{0:T(128)S(1)}, u32[]{:S(2)}, u32[]{:S(2)}) collective-permute-start(f32[96]{0:T(128)S(1)} %pad_maximum_fusion.4), channel_id=1, source_target_pairs={{0,2},{2,4},{4,6},{6,8},{8,10},{10,12},{12,14},{14,16},{16,18},{18... | collective-permute-start | bytes 1160 | tf_op jit(solution)/shard_map/ppermute | solution.py:377
  16.9 12.8 %collective-permute-start.8 = (f32[96]{0:T(128)S(1)}, f32[96]{0:T(128)S(1)}, u32[]{:S(2)}, u32[]{:S(2)}) collective-permute-start(f32[96]{0:T(128)S(1)} %pad_maximum_fusion.4), channel_id=1, source_target_pairs={{2,0},{4,2},{6,4},{8,6},{10,8},{12,10},{14,12},{16,14},{18,16},{20... | collective-permute-start | bytes 1160 | tf_op jit(solution)/shard_map/ppermute | solution.py:378
  29.8 7.5 %collective-permute-start.6 = (f32[3,16,80,128]{3,2,1,0:T(8,128)S(1)}, f32[3,16,80,128]{3,2,1,0:T(8,128)S(1)}, u32[]{:S(2)}, u32[]{:S(2)}) collective-permute-start(f32[3,16,80,128]{3,2,1,0:T(8,128)S(1)} %get-tuple-element.126), channel_id=1, source_target_pairs={{0,1},{1,0},{2,3},{3,2},{4,5},{5,4},{6,7},{7,6},{8,9},{9,8},{10,11... | collective-permute-start | bytes 5898248 | tf_op jit(solution)/shard_map/ppermute | solution.py:358
  32.1 3.7 %collective-permute-start.3 = (f32[15,64,128]{2,1,0:T(8,128)S(1)}, f32[15,64,128]{2,1,0:T(8,128)S(1)}, u32[]{:S(2)}, u32[]{:S(2)}) collective-permute-start(f32[15,64,128]{2,1,0:T(8,128)S(1)} %collective-permute-done.1.first), channel_id=1, source_target_pairs={{0,1},{1,0},{2,3},{3,2},{4,5},{5,4},{6,7},{7,6},{8,9},{9,8},{10,11... | collective-permute-start | bytes 1474568 | tf_op jit(solution)/shard_map/ppermute | solution.py:358
  32.2 3.6 %collective-permute-start.5 = (f32[15,64,128]{2,1,0:T(8,128)S(1)}, f32[15,64,128]{2,1,0:T(8,128)S(1)}, u32[]{:S(2)}, u32[]{:S(2)}) collective-permute-start(f32[15,64,128]{2,1,0:T(8,128)S(1)} %collective-permute-done.2.second), channel_id=1, source_target_pairs={{0,1},{1,0},{2,3},{3,2},{4,5},{5,4},{6,7},{7,6},{8,9},{9,8},{10,11... | collective-permute-start | bytes 1474568 | tf_op jit(solution)/shard_map/ppermute | solution.py:358
  44.0 13.1 %collective-permute-start.11 = (f32[15,32,128]{2,1,0:T(8,128)}, f32[15,32,128]{2,1,0:T(8,128)S(1)}, u32[]{:S(2)}, u32[]{:S(2)}) collective-permute-start(f32[15,32,128]{2,1,0:T(8,128)} %get-tuple-element.134), channel_id=1, source_target_pairs={{2,4},{4,2},{6,8},{8,6},{10,12},{12,10},{14,16},{16,14},{18,20},{2... | collective-permute-start | bytes 737288 | tf_op jit(solution)/shard_map/ppermute | solution.py:354
  47.6 9.5 %collective-permute-start.12 = (f32[15,32,128]{2,1,0:T(8,128)}, f32[15,32,128]{2,1,0:T(8,128)S(1)}, u32[]{:S(2)}, u32[]{:S(2)}) collective-permute-start(f32[15,32,128]{2,1,0:T(8,128)} %get-tuple-element.135), channel_id=1, source_target_pairs={{0,2},{2,0},{4,6},{6,4},{8,10},{10,8},{12,14},{14,12},{16,18},{18,... | collective-permute-start | bytes 737288 | tf_op jit(solution)/shard_map/ppermute | solution.py:354
  47.7 13.7 %collective-permute-start.10 = (f32[15,32,128]{2,1,0:T(8,128)}, f32[15,32,128]{2,1,0:T(8,128)S(1)}, u32[]{:S(2)}, u32[]{:S(2)}) collective-permute-start(f32[15,32,128]{2,1,0:T(8,128)} %copy-done.10), channel_id=1, source_target_pairs={{0,2},{2,0},{4,6},{6,4},{8,10},{10,8},{12,14},{14,12},{16,18},{18,... | collective-permute-start | bytes 737288 | tf_op jit(solution)/shard_map/ppermute | solution.py:354
  49.2 12.5 %collective-permute-start.9 = (f32[15,32,128]{2,1,0:T(8,128)S(1)}, f32[15,32,128]{2,1,0:T(8,128)S(1)}, u32[]{:S(2)}, u32[]{:S(2)}) collective-permute-start(f32[15,32,128]{2,1,0:T(8,128)S(1)} %get-tuple-element.131), channel_id=1, source_target_pairs={{2,4},{4,2},{6,8},{8,6},{10,12},{12,10},{14,16},{16,14},{18,20},{2... | collective-permute-start | bytes 737288 | tf_op jit(solution)/shard_map/ppermute | solution.py:354
  57.8 11.8 %collective-permute-start.13 = (f32[15,32,128]{2,1,0:T(8,128)S(1)}, f32[15,32,128]{2,1,0:T(8,128)S(1)}, u32[]{:S(2)}, u32[]{:S(2)}) collective-permute-start(f32[15,32,128]{2,1,0:T(8,128)S(1)} %get-tuple-element.140), channel_id=1, source_target_pairs={{2,4},{4,2},{6,8},{8,6},{10,12},{12,10},{14,16},{16,14},{18,20},{2... | collective-permute-start | bytes 737288 | tf_op jit(solution)/shard_map/ppermute | solution.py:354
  61.4 10.3 %collective-permute-start.16 = (f32[15,32,128]{2,1,0:T(8,128)S(1)}, f32[15,32,128]{2,1,0:T(8,128)S(1)}, u32[]{:S(2)}, u32[]{:S(2)}) collective-permute-start(f32[15,32,128]{2,1,0:T(8,128)S(1)} %get-tuple-element.142), channel_id=1, source_target_pairs={{0,2},{2,0},{4,6},{6,4},{8,10},{10,8},{12,14},{14,12},{16,18},{18,... | collective-permute-start | bytes 737288 | tf_op jit(solution)/shard_map/ppermute | solution.py:354
  61.7 11.5 %collective-permute-start.15 = (f32[16,32,128]{2,1,0:T(8,128)S(1)}, f32[16,32,128]{2,1,0:T(8,128)S(1)}, u32[]{:S(2)}, u32[]{:S(2)}) collective-permute-start(f32[16,32,128]{2,1,0:T(8,128)S(1)} %get-tuple-element.141.own.current), channel_id=1, source_target_pairs={{0,1},{1,0},{2,3},{3,2},{4,5},{5,4},{6,7},{7,6},{8,9},{9,8},{10,11... | collective-permute-start | bytes 786440 | tf_op jit(solution)/shard_map/ppermute | solution.py:358
  64.0 13.3 %collective-permute-start.18 = (f32[15,32,128]{2,1,0:T(8,128)S(1)}, f32[15,32,128]{2,1,0:T(8,128)S(1)}, u32[]{:S(2)}, u32[]{:S(2)}) collective-permute-start(f32[15,32,128]{2,1,0:T(8,128)S(1)} %get-tuple-element.148), channel_id=1, source_target_pairs={{2,4},{4,2},{6,8},{8,6},{10,12},{12,10},{14,16},{16,14},{18,20},{2... | collective-permute-start | bytes 737288 | tf_op jit(solution)/shard_map/ppermute | solution.py:354
  67.8 9.5 %collective-permute-start.19 = (f32[15,32,128]{2,1,0:T(8,128)S(1)}, f32[15,32,128]{2,1,0:T(8,128)S(1)}, u32[]{:S(2)}, u32[]{:S(2)}) collective-permute-start(f32[15,32,128]{2,1,0:T(8,128)S(1)} %get-tuple-element.149), channel_id=1, source_target_pairs={{0,2},{2,0},{4,6},{6,4},{8,10},{10,8},{12,14},{14,12},{16,18},{18,... | collective-permute-start | bytes 737288 | tf_op jit(solution)/shard_map/ppermute | solution.py:354
  69.6 3.6 %collective-permute-start.14 = (f32[15,32,128]{2,1,0:T(8,128)S(1)}, f32[15,32,128]{2,1,0:T(8,128)S(1)}, u32[]{:S(2)}, u32[]{:S(2)}) collective-permute-start(f32[15,32,128]{2,1,0:T(8,128)S(1)} %collective-permute-done.13.first), channel_id=1, source_target_pairs={{0,1},{1,0},{2,3},{3,2},{4,5},{5,4},{6,7},{7,6},{8,9},{9,8},{10,11... | collective-permute-start | bytes 737288 | tf_op jit(solution)/shard_map/ppermute | solution.py:358
  71.7 1.6 collective-permute-start.17
  84.2 12.2 %collective-permute-start.22 = (f32[15,32,128]{2,1,0:T(8,128)S(1)}, f32[15,32,128]{2,1,0:T(8,128)S(1)}, u32[]{:S(2)}, u32[]{:S(2)}) collective-permute-start(f32[15,32,128]{2,1,0:T(8,128)S(1)} %get-tuple-element.158), channel_id=1, source_target_pairs={{2,4},{4,2},{6,8},{8,6},{10,12},{12,10},{14,16},{16,14},{18,20},{2... | collective-permute-start | bytes 737288 | tf_op jit(solution)/shard_map/ppermute | solution.py:354
  87.8 8.6 %collective-permute-start.23 = (f32[15,32,128]{2,1,0:T(8,128)S(1)}, f32[15,32,128]{2,1,0:T(8,128)S(1)}, u32[]{:S(2)}, u32[]{:S(2)}) collective-permute-start(f32[15,32,128]{2,1,0:T(8,128)S(1)} %get-tuple-element.159), channel_id=1, source_target_pairs={{0,2},{2,0},{4,6},{6,4},{8,10},{10,8},{12,14},{14,12},{16,18},{18,... | collective-permute-start | bytes 737288 | tf_op jit(solution)/shard_map/ppermute | solution.py:354
  87.8 13.9 %collective-permute-start.20 = (f32[15,32,128]{2,1,0:T(8,128)S(1)}, f32[15,32,128]{2,1,0:T(8,128)S(1)}, u32[]{:S(2)}, u32[]{:S(2)}) collective-permute-start(f32[15,32,128]{2,1,0:T(8,128)S(1)} %get-tuple-element.155), channel_id=1, source_target_pairs={{2,4},{4,2},{6,8},{8,6},{10,12},{12,10},{14,16},{16,14},{18,20},{2... | collective-permute-start | bytes 737288 | tf_op jit(solution)/shard_map/ppermute | solution.py:354
  91.2 10.5 %collective-permute-start.21 = (f32[15,32,128]{2,1,0:T(8,128)S(1)}, f32[15,32,128]{2,1,0:T(8,128)S(1)}, u32[]{:S(2)}, u32[]{:S(2)}) collective-permute-start(f32[15,32,128]{2,1,0:T(8,128)S(1)} %get-tuple-element.156), channel_id=1, source_target_pairs={{0,2},{2,0},{4,6},{6,4},{8,10},{10,8},{12,14},{14,12},{16,18},{18,... | collective-permute-start | bytes 737288 | tf_op jit(solution)/shard_map/ppermute | solution.py:354
  97.1 11.1 %collective-permute-start.24 = (f32[15,32,128]{2,1,0:T(8,128)S(1)}, f32[15,32,128]{2,1,0:T(8,128)S(1)}, u32[]{:S(2)}, u32[]{:S(2)}) collective-permute-start(f32[15,32,128]{2,1,0:T(8,128)S(1)} %get-tuple-element.164), channel_id=1, source_target_pairs={{2,4},{4,2},{6,8},{8,6},{10,12},{12,10},{14,16},{16,14},{18,20},{2... | collective-permute-start | bytes 737288 | tf_op jit(solution)/shard_map/ppermute | solution.py:354
  100.7 11.1 %collective-permute-start.27 = (f32[15,32,128]{2,1,0:T(8,128)S(1)}, f32[15,32,128]{2,1,0:T(8,128)S(1)}, u32[]{:S(2)}, u32[]{:S(2)}) collective-permute-start(f32[15,32,128]{2,1,0:T(8,128)S(1)} %get-tuple-element.166), channel_id=1, source_target_pairs={{0,2},{2,0},{4,6},{6,4},{8,10},{10,8},{12,14},{14,12},{16,18},{18,... | collective-permute-start | bytes 737288 | tf_op jit(solution)/shard_map/ppermute | solution.py:354
  101.7 11.6 %collective-permute-start.26 = (f32[16,32,128]{2,1,0:T(8,128)S(1)}, f32[16,32,128]{2,1,0:T(8,128)S(1)}, u32[]{:S(2)}, u32[]{:S(2)}) collective-permute-start(f32[16,32,128]{2,1,0:T(8,128)S(1)} %get-tuple-element.165.own.current), channel_id=1, source_target_pairs={{0,1},{1,0},{2,3},{3,2},{4,5},{5,4},{6,7},{7,6},{8,9},{9,8},{10,11... | collective-permute-start | bytes 786440 | tf_op jit(solution)/shard_map/ppermute | solution.py:358
  104.7 13.1 %collective-permute-start.29 = (f32[15,32,128]{2,1,0:T(8,128)S(1)}, f32[15,32,128]{2,1,0:T(8,128)S(1)}, u32[]{:S(2)}, u32[]{:S(2)}) collective-permute-start(f32[15,32,128]{2,1,0:T(8,128)S(1)} %get-tuple-element.172), channel_id=1, source_target_pairs={{2,4},{4,2},{6,8},{8,6},{10,12},{12,10},{14,16},{16,14},{18,20},{2... | collective-permute-start | bytes 737288 | tf_op jit(solution)/shard_map/ppermute | solution.py:354
  108.2 9.6 %collective-permute-start.30 = (f32[15,32,128]{2,1,0:T(8,128)S(1)}, f32[15,32,128]{2,1,0:T(8,128)S(1)}, u32[]{:S(2)}, u32[]{:S(2)}) collective-permute-start(f32[15,32,128]{2,1,0:T(8,128)S(1)} %get-tuple-element.173), channel_id=1, source_target_pairs={{0,2},{2,0},{4,6},{6,4},{8,10},{10,8},{12,14},{14,12},{16,18},{18,... | collective-permute-start | bytes 737288 | tf_op jit(solution)/shard_map/ppermute | solution.py:354
  108.2 5.1 %collective-permute-start.25 = (f32[15,32,128]{2,1,0:T(8,128)S(1)}, f32[15,32,128]{2,1,0:T(8,128)S(1)}, u32[]{:S(2)}, u32[]{:S(2)}) collective-permute-start(f32[15,32,128]{2,1,0:T(8,128)S(1)} %collective-permute-done.24.first), channel_id=1, source_target_pairs={{0,1},{1,0},{2,3},{3,2},{4,5},{5,4},{6,7},{7,6},{8,9},{9,8},{10,11... | collective-permute-start | bytes 737288 | tf_op jit(solution)/shard_map/ppermute | solution.py:358
  111.7 1.6 collective-permute-start.28
  124.6 12.2 %collective-permute-start.33 = (f32[15,32,128]{2,1,0:T(8,128)S(1)}, f32[15,32,128]{2,1,0:T(8,128)S(1)}, u32[]{:S(2)}, u32[]{:S(2)}) collective-permute-start(f32[15,32,128]{2,1,0:T(8,128)S(1)} %get-tuple-element.182), channel_id=1, source_target_pairs={{2,4},{4,2},{6,8},{8,6},{10,12},{12,10},{14,16},{16,14},{18,20},{2... | collective-permute-start | bytes 737288 | tf_op jit(solution)/shard_map/ppermute | solution.py:354
  128.1 8.8 %collective-permute-start.34 = (f32[15,32,128]{2,1,0:T(8,128)S(1)}, f32[15,32,128]{2,1,0:T(8,128)S(1)}, u32[]{:S(2)}, u32[]{:S(2)}) collective-permute-start(f32[15,32,128]{2,1,0:T(8,128)S(1)} %get-tuple-element.183), channel_id=1, source_target_pairs={{0,2},{2,0},{4,6},{6,4},{8,10},{10,8},{12,14},{14,12},{16,18},{18,... | collective-permute-start | bytes 737288 | tf_op jit(solution)/shard_map/ppermute | solution.py:354
  128.1 14.0 %collective-permute-start.31 = (f32[15,32,128]{2,1,0:T(8,128)S(1)}, f32[15,32,128]{2,1,0:T(8,128)S(1)}, u32[]{:S(2)}, u32[]{:S(2)}) collective-permute-start(f32[15,32,128]{2,1,0:T(8,128)S(1)} %get-tuple-element.179), channel_id=1, source_target_pairs={{2,4},{4,2},{6,8},{8,6},{10,12},{12,10},{14,16},{16,14},{18,20},{2... | collective-permute-start | bytes 737288 | tf_op jit(solution)/shard_map/ppermute | solution.py:354
  131.6 10.5 %collective-permute-start.32 = (f32[15,32,128]{2,1,0:T(8,128)S(1)}, f32[15,32,128]{2,1,0:T(8,128)S(1)}, u32[]{:S(2)}, u32[]{:S(2)}) collective-permute-start(f32[15,32,128]{2,1,0:T(8,128)S(1)} %get-tuple-element.180), channel_id=1, source_target_pairs={{0,2},{2,0},{4,6},{6,4},{8,10},{10,8},{12,14},{14,12},{16,18},{18,... | collective-permute-start | bytes 737288 | tf_op jit(solution)/shard_map/ppermute | solution.py:354
  137.5 11.1 %collective-permute-start.35 = (f32[15,32,128]{2,1,0:T(8,128)S(1)}, f32[15,32,128]{2,1,0:T(8,128)S(1)}, u32[]{:S(2)}, u32[]{:S(2)}) collective-permute-start(f32[15,32,128]{2,1,0:T(8,128)S(1)} %get-tuple-element.188), channel_id=1, source_target_pairs={{2,4},{4,2},{6,8},{8,6},{10,12},{12,10},{14,16},{16,14},{18,20},{2... | collective-permute-start | bytes 737288 | tf_op jit(solution)/shard_map/ppermute | solution.py:354
  141.0 11.2 %collective-permute-start.38 = (f32[15,32,128]{2,1,0:T(8,128)S(1)}, f32[15,32,128]{2,1,0:T(8,128)S(1)}, u32[]{:S(2)}, u32[]{:S(2)}) collective-permute-start(f32[15,32,128]{2,1,0:T(8,128)S(1)} %get-tuple-element.190), channel_id=1, source_target_pairs={{0,2},{2,0},{4,6},{6,4},{8,10},{10,8},{12,14},{14,12},{16,18},{18,... | collective-permute-start | bytes 737288 | tf_op jit(solution)/shard_map/ppermute | solution.py:354
  142.1 11.7 %collective-permute-start.37 = (f32[16,32,128]{2,1,0:T(8,128)S(1)}, f32[16,32,128]{2,1,0:T(8,128)S(1)}, u32[]{:S(2)}, u32[]{:S(2)}) collective-permute-start(f32[16,32,128]{2,1,0:T(8,128)S(1)} %get-tuple-element.189.own.current), channel_id=1, source_target_pairs={{0,1},{1,0},{2,3},{3,2},{4,5},{5,4},{6,7},{7,6},{8,9},{9,8},{10,11... | collective-permute-start | bytes 786440 | tf_op jit(solution)/shard_map/ppermute | solution.py:358
  145.0 13.1 %collective-permute-start.40 = (f32[15,32,128]{2,1,0:T(8,128)S(1)}, f32[15,32,128]{2,1,0:T(8,128)S(1)}, u32[]{:S(2)}, u32[]{:S(2)}) collective-permute-start(f32[15,32,128]{2,1,0:T(8,128)S(1)} %get-tuple-element.196), channel_id=1, source_target_pairs={{2,4},{4,2},{6,8},{8,6},{10,12},{12,10},{14,16},{16,14},{18,20},{2... | collective-permute-start | bytes 737288 | tf_op jit(solution)/shard_map/ppermute | solution.py:354
  148.6 9.5 %collective-permute-start.41 = (f32[15,32,128]{2,1,0:T(8,128)S(1)}, f32[15,32,128]{2,1,0:T(8,128)S(1)}, u32[]{:S(2)}, u32[]{:S(2)}) collective-permute-start(f32[15,32,128]{2,1,0:T(8,128)S(1)} %get-tuple-element.197), channel_id=1, source_target_pairs={{0,2},{2,0},{4,6},{6,4},{8,10},{10,8},{12,14},{14,12},{16,18},{18,... | collective-permute-start | bytes 737288 | tf_op jit(solution)/shard_map/ppermute | solution.py:354
  148.6 5.1 %collective-permute-start.36 = (f32[15,32,128]{2,1,0:T(8,128)S(1)}, f32[15,32,128]{2,1,0:T(8,128)S(1)}, u32[]{:S(2)}, u32[]{:S(2)}) collective-permute-start(f32[15,32,128]{2,1,0:T(8,128)S(1)} %collective-permute-done.35.first), channel_id=1, source_target_pairs={{0,1},{1,0},{2,3},{3,2},{4,5},{5,4},{6,7},{7,6},{8,9},{9,8},{10,11... | collective-permute-start | bytes 737288 | tf_op jit(solution)/shard_map/ppermute | solution.py:358
  152.2 1.6 collective-permute-start.39
  164.9 12.2 %collective-permute-start.44 = (f32[15,32,128]{2,1,0:T(8,128)S(1)}, f32[15,32,128]{2,1,0:T(8,128)S(1)}, u32[]{:S(2)}, u32[]{:S(2)}) collective-permute-start(f32[15,32,128]{2,1,0:T(8,128)S(1)} %get-tuple-element.206), channel_id=1, source_target_pairs={{2,4},{4,2},{6,8},{8,6},{10,12},{12,10},{14,16},{16,14},{18,20},{2... | collective-permute-start | bytes 737288 | tf_op jit(solution)/shard_map/ppermute | solution.py:354
  168.5 8.6 %collective-permute-start.45 = (f32[15,32,128]{2,1,0:T(8,128)S(1)}, f32[15,32,128]{2,1,0:T(8,128)S(1)}, u32[]{:S(2)}, u32[]{:S(2)}) collective-permute-start(f32[15,32,128]{2,1,0:T(8,128)S(1)} %get-tuple-element.207), channel_id=1, source_target_pairs={{0,2},{2,0},{4,6},{6,4},{8,10},{10,8},{12,14},{14,12},{16,18},{18,... | collective-permute-start | bytes 737288 | tf_op jit(solution)/shard_map/ppermute | solution.py:354
  168.5 13.8 %collective-permute-start.42 = (f32[15,32,128]{2,1,0:T(8,128)S(1)}, f32[15,32,128]{2,1,0:T(8,128)S(1)}, u32[]{:S(2)}, u32[]{:S(2)}) collective-permute-start(f32[15,32,128]{2,1,0:T(8,128)S(1)} %get-tuple-element.203), channel_id=1, source_target_pairs={{2,4},{4,2},{6,8},{8,6},{10,12},{12,10},{14,16},{16,14},{18,20},{2... | collective-permute-start | bytes 737288 | tf_op jit(solution)/shard_map/ppermute | solution.py:354
  171.9 10.5 %collective-permute-start.43 = (f32[15,32,128]{2,1,0:T(8,128)S(1)}, f32[15,32,128]{2,1,0:T(8,128)S(1)}, u32[]{:S(2)}, u32[]{:S(2)}) collective-permute-start(f32[15,32,128]{2,1,0:T(8,128)S(1)} %get-tuple-element.204), channel_id=1, source_target_pairs={{0,2},{2,0},{4,6},{6,4},{8,10},{10,8},{12,14},{14,12},{16,18},{18,... | collective-permute-start | bytes 737288 | tf_op jit(solution)/shard_map/ppermute | solution.py:354
  182.4 2.9 %collective-permute-start.47 = (f32[16,32,128]{2,1,0:T(8,128)S(1)}, f32[16,32,128]{2,1,0:T(8,128)S(1)}, u32[]{:S(2)}, u32[]{:S(2)}) collective-permute-start(f32[16,32,128]{2,1,0:T(8,128)S(1)} %update.14), channel_id=1, source_target_pairs={{0,1},{1,0},{2,3},{3,2},{4,5},{5,4},{6,7},{7,6},{8,9},{9,8},{10,11... | collective-permute-start | bytes 786440 | tf_op jit(solution)/shard_map/ppermute | solution.py:358
  184.7 1.6 collective-permute-start.46
  (12 other events, 60.9 us)

commit v2 on v1

--- a/solution.py
+++ b/solution.py
@@ -61,6 +61,15 @@
     ref[lead + (pl.ds(rows, rows),)] = low
 
 
+def three(value, column, width):
+    high = value.astype(BF16).astype(F32)
+    return jnp.where((column >= width) & (column < 2 * width), value - high, high).astype(BF16)
+
+
+def thirds(column, width):
+    return column - jnp.where(column >= 2 * width, 2 * width, jnp.where(column >= width, width, 0))
+
+
 def select(taps, view, axis, index):
     total = jnp.zeros(index.shape, F32)
     for k in range(TAPS):
@@ -76,16 +85,16 @@
 def matrices_kernel(where, taps, xf, yf, yt, zf, zt):
     core, tile, odd = where[0], where[1], where[2]
 
-    shape = (VIEWS * W, 2 * SLOTS)
-    slot = iota(shape, 1)
-    slot = jnp.where(slot < SLOTS, slot, slot - SLOTS)
+    shape = (VIEWS * W, 3 * SLOTS)
+    column = iota(shape, 1)
+    slot = thirds(column, SLOTS)
     plane = plane_of(slot, odd)
     row = iota(shape, 0)
     index = jnp.where(in_grid(slot, plane, tile), plane - row % W + REACH, -1)
     total = jnp.zeros(shape, F32)
     for view in range(VIEWS):
         total = jnp.where(row // W == view, select(taps, view, 0, index), total)
-    put(xf, (), VIEWS * W, total)
+    xf[...] = three(total, column, SLOTS)
 
     def per_view(view, _):
         shape = (MID, 2 * EXT)
@@ -93,11 +102,11 @@
         j = jnp.where(j < EXT, j, j - EXT)
         index = row_of(j, core) - mid_row_of(iota(shape, 0), core) + REACH
         put(yf, (view,), MID, select(taps, view, 1, index))
-        shape = (HALF, 2 * MID)
-        j = iota(shape, 1)
-        j = jnp.where(j < MID, j, j - MID)
+        shape = (HALF, 3 * MID)
+        column = iota(shape, 1)
+        j = thirds(column, MID)
         index = row_of(iota(shape, 0), core) - mid_row_of(j, core) + REACH
-        put(yt, (view,), HALF, select(taps, view, 1, index))
+        yt[view] = three(select(taps, view, 1, index), column, MID)
         difference = iota((NZ, NZ), 0) - iota((NZ, NZ), 1)
         for ref, sign in ((zf, 1), (zt, -1)):
             high, low = split(select(taps, view, 2, sign * difference + REACH))
@@ -111,9 +120,9 @@
 
 def make_matrices(where, taps):
     shapes = [
-        (2 * VIEWS * W, 2 * SLOTS),
+        (VIEWS * W, 3 * SLOTS),
         (VIEWS, 2 * MID, 2 * EXT),
-        (VIEWS, 2 * HALF, 2 * MID),
+        (VIEWS, HALF, 3 * MID),
         (VIEWS, 2 * NZ, 2 * NZ),
         (VIEWS, 2 * NZ, 2 * NZ),
     ]
@@ -170,13 +179,16 @@
     return jnp.concatenate(blocks, 1)
 
 
-def along_x(source, target, matrix, rows, taken, given, source_step, target_step):
+def along_x(source, target, matrix, rows, taken, given, source_step, target_step, products):
     group = 16
 
     def body(step, _):
         parts = [split(source[pl.ds(step * group + i, taken, stride=source_step)]) for i in range(group)]
-        operand = jnp.concatenate([beside([p[0] for p in parts]), beside([p[1] for p in parts])], 0)
-        result = both(dot(matrix[...], operand))
+        high, low = beside([p[0] for p in parts]), beside([p[1] for p in parts])
+        if products == 3:
+            result = dot(matrix[...], jnp.concatenate([high, high, low], 0))
+        else:
+            result = both(dot(matrix[...], jnp.concatenate([high, low], 0)))
         for i in range(group):
             target[pl.ds(step * group + i, given, stride=target_step)] = result[:, i * NZ : (i + 1) * NZ]
         return 0
@@ -193,7 +205,7 @@
     while slot < SLOTS:
         ext[pl.ds(slot * PART_STEP, PART)] = jnp.zeros((PART, NZ), F32)
         slot += 1
-    along_x(ext, mid, xf, PART, SLOTS, VIEWS * W, PART_STEP, PART_STEP)
+    along_x(ext, mid, xf, PART, SLOTS, VIEWS * W, PART_STEP, PART_STEP, 3)
 
     def along_z(view, _):
         start = pl.multiple_of(view * (W * PART_STEP), 16)
@@ -234,7 +246,8 @@
             )
             blurred = both(dot(yf[view], operand))
             measured = beside([data[step, i] for i in range(W)])
-            result = both(dot(yt[view], jnp.concatenate(split(measured / blurred), 0)))
+            high, low = split(measured / blurred)
+            result = dot(yt[view], jnp.concatenate([high, high, low], 0))
             block = jnp.concatenate([result[:, i * NZ : (i + 1) * NZ] for i in range(W)], 0)
             block = pair(dot(beside(split(block)), zt[view]))
             start = pl.multiple_of(view * (W * OWN_STEP), 16)
@@ -246,7 +259,7 @@
 
     inner(mine, 0, 3)
     inner(theirs, VIEWS // 2, 1)
-    along_x(back, wide, xt, HALF, VIEWS * W, SLOTS, OWN_STEP, OWN_STEP)
+    along_x(back, wide, xt, HALF, VIEWS * W, SLOTS, OWN_STEP, OWN_STEP, 4)
     for at, outs in ((0, (near1, near_own, near2)), (PART, (far1, far_own, far2))):
         for slot, out in zip((0, 15, 31), outs):
             for i in range(out.shape[0]):

time: 188 us -> 187 us (level)
    pallas_call x12, Pallas kernels: 18.3 us -> 16.2 us  [blur(): pl.pallas_call(functools.partial(blur_kernel, at), out_shape=[jax.ShapeDt...]
  transfers between devices with their start and end apart: 48 -> 48, of which waited for: 14 -> 18; matrix products, arithmetic and copies ran while one was open for 0% -> 0% of each run, Pallas kernels for 14% -> 13%
where the time goes in v2:
time: 187 us
  starting transfers between devices  86.9 us (46%)
  Pallas kernels  52.7 us (28%)
  waiting for transfers between devices  39.4 us (21%)
  local copies, waits for them, and re-layouts  4.21 us (2%)
  other arithmetic  3.1 us (2%)
    ppermute x30, starting transfers between devices, exchange(): return lax.ppermute(x, 'tile', pairs)  59.1 us
    ppermute x30, waiting for transfers between devices, exchange(): return lax.ppermute(x, 'tile', pairs)  37.4 us
    pallas_call x4, Pallas kernels, correct(): pl.pallas_call(correct_kernel, out_shape=[jax.ShapeDtypeStruct(s, F32) fo...  22.3 us
    ppermute x16, starting transfers between devices, swap(): return lax.ppermute(x, 'view', [(0, 1), (1, 0)])  20.8 us
    pallas_call x12, Pallas kernels, blur(): pl.pallas_call(functools.partial(blur_kernel, at), out_shape=[jax.ShapeDt...  16.2 us
    pallas_call x8, Pallas kernels, update(): pl.pallas_call(add_neighbours if last else update_kernel, out_shape=[jax....  5.52 us
    ppermute x1, starting transfers between devices, per_device(): after = lax.ppermute(cover, 'tile', [(j, i) for i, j in ring])  5.15 us
    pallas_call x1, Pallas kernels, make_matrices(): pl.pallas_call(matrices_kernel, out_shape=[jax.ShapeDtypeStruct(s, BF16)...  4.85 us
  transfers between devices with their start and end apart: 48, of which 18 were waited for; matrix products, arithmetic and copies ran while one was open for 0% of the time, Pallas kernels for 13%

profile of v2, /device:TPU:1, one launch (start us, length us, event | category | flops | bytes accessed | tf_op | source)
XLA Modules:
  0.0 186.8 jit_solution(9201500893992037427)
XLA Ops:
  1.3 1.6 begin.1
  4.7 1.4 collective-permute-start
  6.1 8.5 %collective-permute-start.1 = (f32[15,64,128]{2,1,0:T(8,128)}, f32[15,64,128]{2,1,0:T(8,128)S(1)}, u32[]{:S(2)}, u32[]{:S(2)}) collective-permute-start(f32[15,64,128]{2,1,0:T(8,128)} %get-tuple-element.114), channel_id=1, source_target_pairs={{2,4},{4,2},{6,8},{8,6},{10,12},{12,10},{14,16},{16,14},{18,20},{2... | collective-permute-start | bytes 1474568 | tf_op jit(solution)/shard_map/ppermute | solution.py:367
  15.1 1.7 collective-permute-start.7
  16.9 5.2 %collective-permute-start.8 = (f32[96]{0:T(128)S(1)}, f32[96]{0:T(128)S(1)}, u32[]{:S(2)}, u32[]{:S(2)}) collective-permute-start(f32[96]{0:T(128)S(1)} %pad_maximum_fusion.4), channel_id=1, source_target_pairs={{2,0},{4,2},{6,4},{8,6},{10,8},{12,10},{14,12},{16,14},{18,16},{20... | collective-permute-start | bytes 1160 | tf_op jit(solution)/shard_map/ppermute | solution.py:391
  22.1 4.8 %matrices.1 = (bf16[96,144]{1,0:T(8,128)(2,1)S(1)}, bf16[6,160,192]{2,1,0:T(8,128)(2,1)S(1)}, bf16[6,64,240]{2,1,0:T(8,128)(2,1)S(1)}, bf16[6,256,256]{2,1,0:T(8,128)(2,1)S(1)}, bf16[6,256,256]{2,1,0:T(8,128)(2,1)S(1)}) custom-call(s32[3]{0:T(128)S(1)} %pad_add_fusion.where, f32[558]{0:T(1024)S(1)} %pad_maximum_fusion.1.taps), custom_call_target="tpu_custom_call" | custom-call | flops 1000 | bytes 1000 | tf_op jit(solution)/shard_map/matrices/pallas_call | solution.py:129
  27.0 1.9 %copy-done = f32[3,16,128,128]{3,2,1,0:T(8,128)S(1)} copy-done((f32[3,16,128,128]{3,2,1,0:T(8,128)S(1)}, f32[3,16,128,128]{3,2,1,0:T(8,128)}, u32[]{:S(2)}) %copy-start) | copy-done | bytes 3145752
  30.6 1.6 cover_matrix.1.xt
  32.7 1.4 blur.13
  37.0 6.1 %correct.4 = (f32[15,32,128]{2,1,0:T(8,128)}, f32[16,32,128]{2,1,0:T(8,128)S(1)}, f32[15,32,128]{2,1,0:T(8,128)}, f32[15,32,128]{2,1,0:T(8,128)S(1)}, f32[16,32,...) custom-call(bf16[96,32,128]{2,1,0:T(8,128)(2,1)S(1)} %get-tuple-element.118.near_high, ...), custom_call_target="tpu_custom_call" | custom-call | flops 4000000000 | bytes 16000000 | tf_op jit(solution)/shard_map/correct/pallas_call | solution.py:273
  43.8 3.5 %collective-permute-start.11 = (f32[15,32,128]{2,1,0:T(8,128)}, f32[15,32,128]{2,1,0:T(8,128)S(1)}, u32[]{:S(2)}, u32[]{:S(2)}) collective-permute-start(f32[15,32,128]{2,1,0:T(8,128)} %get-tuple-element.134), channel_id=1, source_target_pairs={{2,4},{4,2},{6,8},{8,6},{10,12},{12,10},{14,16},{16,14},{18,20},{2... | collective-permute-start | bytes 737288 | tf_op jit(solution)/shard_map/ppermute | solution.py:367
  47.4 1.5 collective-permute-start.10
  48.9 3.4 %collective-permute-start.9 = (f32[15,32,128]{2,1,0:T(8,128)S(1)}, f32[15,32,128]{2,1,0:T(8,128)S(1)}, u32[]{:S(2)}, u32[]{:S(2)}) collective-permute-start(f32[15,32,128]{2,1,0:T(8,128)S(1)} %get-tuple-element.131), channel_id=1, source_target_pairs={{2,4},{4,2},{6,8},{8,6},{10,12},{12,10},{14,16},{16,14},{18,20},{2... | collective-permute-start | bytes 737288 | tf_op jit(solution)/shard_map/ppermute | solution.py:367
  52.3 4.2 %collective-permute-done.11.from1 = f32[15,32,128]{2,1,0:T(8,128)S(1)} collective-permute-done((f32[15,32,128]{2,1,0:T(8,128)}, f32[15,32,128]{2,1,0:T(8,128)S(1)}, u32[]{:S(2)}, u32[]{:S(2)}) %collective-permute-start.11) | collective-permute-done | bytes 245792 | tf_op jit(solution)/shard_map/ppermute | solution.py:367
  57.3 3.6 %collective-permute-start.13 = (f32[15,32,128]{2,1,0:T(8,128)S(1)}, f32[15,32,128]{2,1,0:T(8,128)S(1)}, u32[]{:S(2)}, u32[]{:S(2)}) collective-permute-start(f32[15,32,128]{2,1,0:T(8,128)S(1)} %get-tuple-element.140), channel_id=1, source_target_pairs={{2,4},{4,2},{6,8},{8,6},{10,12},{12,10},{14,16},{16,14},{18,20},{2... | collective-permute-start | bytes 737288 | tf_op jit(solution)/shard_map/ppermute | solution.py:367
  61.2 1.8 collective-permute-start.15
  63.8 3.6 %collective-permute-start.18 = (f32[15,32,128]{2,1,0:T(8,128)S(1)}, f32[15,32,128]{2,1,0:T(8,128)S(1)}, u32[]{:S(2)}, u32[]{:S(2)}) collective-permute-start(f32[15,32,128]{2,1,0:T(8,128)S(1)} %get-tuple-element.148), channel_id=1, source_target_pairs={{2,4},{4,2},{6,8},{8,6},{10,12},{12,10},{14,16},{16,14},{18,20},{2... | collective-permute-start | bytes 737288 | tf_op jit(solution)/shard_map/ppermute | solution.py:367
  67.3 1.5 collective-permute-done.13.first
  68.8 2.4 %collective-permute-start.14 = (f32[15,32,128]{2,1,0:T(8,128)S(1)}, f32[15,32,128]{2,1,0:T(8,128)S(1)}, u32[]{:S(2)}, u32[]{:S(2)}) collective-permute-start(f32[15,32,128]{2,1,0:T(8,128)S(1)} %collective-permute-done.13.first), channel_id=1, source_target_pairs={{0,1},{1,0},{2,3},{3,2},{4,5},{5,4},{6,7},{7,6},{8,9},{9,8},{10,11... | collective-permute-start | bytes 737288 | tf_op jit(solution)/shard_map/ppermute | solution.py:371
  74.1 2.8 %collective-permute-done.18.first = f32[15,32,128]{2,1,0:T(8,128)S(1)} collective-permute-done((f32[15,32,128]{2,1,0:T(8,128)S(1)}, f32[15,32,128]{2,1,0:T(8,128)S(1)}, u32[]{:S(2)}, u32[]{:S(2)}) %collective-permute-start.18) | collective-permute-done | bytes 245792 | tf_op jit(solution)/shard_map/ppermute | solution.py:367
  76.9 1.4 blur.17
  78.3 5.4 %correct.5 = (f32[15,32,128]{2,1,0:T(8,128)S(1)}, f32[16,32,128]{2,1,0:T(8,128)S(1)}, f32[15,32,128]{2,1,0:T(8,128)S(1)}, f32[15,32,128]{2,1,0:T(8,128)S(1)}, f3...) custom-call(bf16[96,32,128]{2,1,0:T(8,128)(2,1)S(1)} %get-tuple-element.146.near_high, ...), custom_call_target="tpu_custom_call" | custom-call | flops 4000000000 | bytes 16000000 | tf_op jit(solution)/shard_map/correct/pallas_call | solution.py:273
  83.7 3.6 %collective-permute-start.22 = (f32[15,32,128]{2,1,0:T(8,128)S(1)}, f32[15,32,128]{2,1,0:T(8,128)S(1)}, u32[]{:S(2)}, u32[]{:S(2)}) collective-permute-start(f32[15,32,128]{2,1,0:T(8,128)S(1)} %get-tuple-element.158), channel_id=1, source_target_pairs={{2,4},{4,2},{6,8},{8,6},{10,12},{12,10},{14,16},{16,14},{18,20},{2... | collective-permute-start | bytes 737288 | tf_op jit(solution)/shard_map/ppermute | solution.py:367
  87.2 3.4 %collective-permute-start.20 = (f32[15,32,128]{2,1,0:T(8,128)S(1)}, f32[15,32,128]{2,1,0:T(8,128)S(1)}, u32[]{:S(2)}, u32[]{:S(2)}) collective-permute-start(f32[15,32,128]{2,1,0:T(8,128)S(1)} %get-tuple-element.155), channel_id=1, source_target_pairs={{2,4},{4,2},{6,8},{8,6},{10,12},{12,10},{14,16},{16,14},{18,20},{2... | collective-permute-start | bytes 737288 | tf_op jit(solution)/shard_map/ppermute | solution.py:367
  90.6 5.2 %collective-permute-done.22.from1 = f32[15,32,128]{2,1,0:T(8,128)S(1)} collective-permute-done((f32[15,32,128]{2,1,0:T(8,128)S(1)}, f32[15,32,128]{2,1,0:T(8,128)S(1)}, u32[]{:S(2)}, u32[]{:S(2)}) %collective-permute-start.22) | collective-permute-done | bytes 245792 | tf_op jit(solution)/shard_map/ppermute | solution.py:367
  96.6 3.6 %collective-permute-start.24 = (f32[15,32,128]{2,1,0:T(8,128)S(1)}, f32[15,32,128]{2,1,0:T(8,128)S(1)}, u32[]{:S(2)}, u32[]{:S(2)}) collective-permute-start(f32[15,32,128]{2,1,0:T(8,128)S(1)} %get-tuple-element.164), channel_id=1, source_target_pairs={{2,4},{4,2},{6,8},{8,6},{10,12},{12,10},{14,16},{16,14},{18,20},{2... | collective-permute-start | bytes 737288 | tf_op jit(solution)/shard_map/ppermute | solution.py:367
  101.1 2.3 %collective-permute-start.26 = (f32[16,32,128]{2,1,0:T(8,128)S(1)}, f32[16,32,128]{2,1,0:T(8,128)S(1)}, u32[]{:S(2)}, u32[]{:S(2)}) collective-permute-start(f32[16,32,128]{2,1,0:T(8,128)S(1)} %get-tuple-element.165.own.current), channel_id=1, source_target_pairs={{0,1},{1,0},{2,3},{3,2},{4,5},{5,4},{6,7},{7,6},{8,9},{9,8},{10,11... | collective-permute-start | bytes 786440 | tf_op jit(solution)/shard_map/ppermute | solution.py:371
  104.2 3.5 %collective-permute-start.29 = (f32[15,32,128]{2,1,0:T(8,128)S(1)}, f32[15,32,128]{2,1,0:T(8,128)S(1)}, u32[]{:S(2)}, u32[]{:S(2)}) collective-permute-start(f32[15,32,128]{2,1,0:T(8,128)S(1)} %get-tuple-element.172), channel_id=1, source_target_pairs={{2,4},{4,2},{6,8},{8,6},{10,12},{12,10},{14,16},{16,14},{18,20},{2... | collective-permute-start | bytes 737288 | tf_op jit(solution)/shard_map/ppermute | solution.py:367
  107.6 3.6 %collective-permute-start.25 = (f32[15,32,128]{2,1,0:T(8,128)S(1)}, f32[15,32,128]{2,1,0:T(8,128)S(1)}, u32[]{:S(2)}, u32[]{:S(2)}) collective-permute-start(f32[15,32,128]{2,1,0:T(8,128)S(1)} %collective-permute-done.24.first), channel_id=1, source_target_pairs={{0,1},{1,0},{2,3},{3,2},{4,5},{5,4},{6,7},{7,6},{8,9},{9,8},{10,11... | collective-permute-start | bytes 737288 | tf_op jit(solution)/shard_map/ppermute | solution.py:371
  111.2 1.4 blur.19
  112.7 1.4 blur.18
  114.1 3.1 %collective-permute-done.29.first = f32[15,32,128]{2,1,0:T(8,128)S(1)} collective-permute-done((f32[15,32,128]{2,1,0:T(8,128)S(1)}, f32[15,32,128]{2,1,0:T(8,128)S(1)}, u32[]{:S(2)}, u32[]{:S(2)}) %collective-permute-start.29) | collective-permute-done | bytes 245792 | tf_op jit(solution)/shard_map/ppermute | solution.py:367
  118.6 5.4 %correct.6 = (f32[15,32,128]{2,1,0:T(8,128)S(1)}, f32[16,32,128]{2,1,0:T(8,128)S(1)}, f32[15,32,128]{2,1,0:T(8,128)S(1)}, f32[15,32,128]{2,1,0:T(8,128)S(1)}, f3...) custom-call(bf16[96,32,128]{2,1,0:T(8,128)(2,1)S(1)} %get-tuple-element.170.near_high, ...), custom_call_target="tpu_custom_call" | custom-call | flops 4000000000 | bytes 16000000 | tf_op jit(solution)/shard_map/correct/pallas_call | solution.py:273
  124.0 3.5 %collective-permute-start.33 = (f32[15,32,128]{2,1,0:T(8,128)S(1)}, f32[15,32,128]{2,1,0:T(8,128)S(1)}, u32[]{:S(2)}, u32[]{:S(2)}) collective-permute-start(f32[15,32,128]{2,1,0:T(8,128)S(1)} %get-tuple-element.182), channel_id=1, source_target_pairs={{2,4},{4,2},{6,8},{8,6},{10,12},{12,10},{14,16},{16,14},{18,20},{2... | collective-permute-start | bytes 737288 | tf_op jit(solution)/shard_map/ppermute | solution.py:367
  127.5 3.5 %collective-permute-start.31 = (f32[15,32,128]{2,1,0:T(8,128)S(1)}, f32[15,32,128]{2,1,0:T(8,128)S(1)}, u32[]{:S(2)}, u32[]{:S(2)}) collective-permute-start(f32[15,32,128]{2,1,0:T(8,128)S(1)} %get-tuple-element.179), channel_id=1, source_target_pairs={{2,4},{4,2},{6,8},{8,6},{10,12},{12,10},{14,16},{16,14},{18,20},{2... | collective-permute-start | bytes 737288 | tf_op jit(solution)/shard_map/ppermute | solution.py:367
  131.0 5.2 %collective-permute-done.33.from1 = f32[15,32,128]{2,1,0:T(8,128)S(1)} collective-permute-done((f32[15,32,128]{2,1,0:T(8,128)S(1)}, f32[15,32,128]{2,1,0:T(8,128)S(1)}, u32[]{:S(2)}, u32[]{:S(2)}) %collective-permute-start.33) | collective-permute-done | bytes 245792 | tf_op jit(solution)/shard_map/ppermute | solution.py:367
  136.9 3.5 %collective-permute-start.35 = (f32[15,32,128]{2,1,0:T(8,128)S(1)}, f32[15,32,128]{2,1,0:T(8,128)S(1)}, u32[]{:S(2)}, u32[]{:S(2)}) collective-permute-start(f32[15,32,128]{2,1,0:T(8,128)S(1)} %get-tuple-element.188), channel_id=1, source_target_pairs={{2,4},{4,2},{6,8},{8,6},{10,12},{12,10},{14,16},{16,14},{18,20},{2... | collective-permute-start | bytes 737288 | tf_op jit(solution)/shard_map/ppermute | solution.py:367
  141.4 2.3 %collective-permute-start.37 = (f32[16,32,128]{2,1,0:T(8,128)S(1)}, f32[16,32,128]{2,1,0:T(8,128)S(1)}, u32[]{:S(2)}, u32[]{:S(2)}) collective-permute-start(f32[16,32,128]{2,1,0:T(8,128)S(1)} %get-tuple-element.189.own.current), channel_id=1, source_target_pairs={{0,1},{1,0},{2,3},{3,2},{4,5},{5,4},{6,7},{7,6},{8,9},{9,8},{10,11... | collective-permute-start | bytes 786440 | tf_op jit(solution)/shard_map/ppermute | solution.py:371
  144.4 3.6 %collective-permute-start.40 = (f32[15,32,128]{2,1,0:T(8,128)S(1)}, f32[15,32,128]{2,1,0:T(8,128)S(1)}, u32[]{:S(2)}, u32[]{:S(2)}) collective-permute-start(f32[15,32,128]{2,1,0:T(8,128)S(1)} %get-tuple-element.196), channel_id=1, source_target_pairs={{2,4},{4,2},{6,8},{8,6},{10,12},{12,10},{14,16},{16,14},{18,20},{2... | collective-permute-start | bytes 737288 | tf_op jit(solution)/shard_map/ppermute | solution.py:367
  148.0 3.6 %collective-permute-start.36 = (f32[15,32,128]{2,1,0:T(8,128)S(1)}, f32[15,32,128]{2,1,0:T(8,128)S(1)}, u32[]{:S(2)}, u32[]{:S(2)}) collective-permute-start(f32[15,32,128]{2,1,0:T(8,128)S(1)} %collective-permute-done.35.first), channel_id=1, source_target_pairs={{0,1},{1,0},{2,3},{3,2},{4,5},{5,4},{6,7},{7,6},{8,9},{9,8},{10,11... | collective-permute-start | bytes 737288 | tf_op jit(solution)/shard_map/ppermute | solution.py:371
  153.1 1.4 blur.21
  154.4 3.0 %collective-permute-done.40.first = f32[15,32,128]{2,1,0:T(8,128)S(1)} collective-permute-done((f32[15,32,128]{2,1,0:T(8,128)S(1)}, f32[15,32,128]{2,1,0:T(8,128)S(1)}, u32[]{:S(2)}, u32[]{:S(2)}) %collective-permute-start.40) | collective-permute-done | bytes 245792 | tf_op jit(solution)/shard_map/ppermute | solution.py:367
  158.8 5.4 %correct.7 = (f32[15,32,128]{2,1,0:T(8,128)S(1)}, f32[16,32,128]{2,1,0:T(8,128)S(1)}, f32[15,32,128]{2,1,0:T(8,128)S(1)}, f32[15,32,128]{2,1,0:T(8,128)S(1)}, f3...) custom-call(bf16[96,32,128]{2,1,0:T(8,128)(2,1)S(1)} %get-tuple-element.194.near_high, ...), custom_call_target="tpu_custom_call" | custom-call | flops 4000000000 | bytes 16000000 | tf_op jit(solution)/shard_map/correct/pallas_call | solution.py:273
  164.2 3.6 %collective-permute-start.44 = (f32[15,32,128]{2,1,0:T(8,128)S(1)}, f32[15,32,128]{2,1,0:T(8,128)S(1)}, u32[]{:S(2)}, u32[]{:S(2)}) collective-permute-start(f32[15,32,128]{2,1,0:T(8,128)S(1)} %get-tuple-element.206), channel_id=1, source_target_pairs={{2,4},{4,2},{6,8},{8,6},{10,12},{12,10},{14,16},{16,14},{18,20},{2... | collective-permute-start | bytes 737288 | tf_op jit(solution)/shard_map/ppermute | solution.py:367
  167.8 3.4 %collective-permute-start.42 = (f32[15,32,128]{2,1,0:T(8,128)S(1)}, f32[15,32,128]{2,1,0:T(8,128)S(1)}, u32[]{:S(2)}, u32[]{:S(2)}) collective-permute-start(f32[15,32,128]{2,1,0:T(8,128)S(1)} %get-tuple-element.203), channel_id=1, source_target_pairs={{2,4},{4,2},{6,8},{8,6},{10,12},{12,10},{14,16},{16,14},{18,20},{2... | collective-permute-start | bytes 737288 | tf_op jit(solution)/shard_map/ppermute | solution.py:367
  171.2 5.2 %collective-permute-done.44.from1 = f32[15,32,128]{2,1,0:T(8,128)S(1)} collective-permute-done((f32[15,32,128]{2,1,0:T(8,128)S(1)}, f32[15,32,128]{2,1,0:T(8,128)S(1)}, u32[]{:S(2)}, u32[]{:S(2)}) %collective-permute-start.44) | collective-permute-done | bytes 245792 | tf_op jit(solution)/shard_map/ppermute | solution.py:367
  177.1 4.6 %collective-permute-done.42.from1 = f32[15,32,128]{2,1,0:T(8,128)S(1)} collective-permute-done((f32[15,32,128]{2,1,0:T(8,128)S(1)}, f32[15,32,128]{2,1,0:T(8,128)S(1)}, u32[]{:S(2)}, u32[]{:S(2)}) %collective-permute-start.42) | collective-permute-done | bytes 245792 | tf_op jit(solution)/shard_map/ppermute | solution.py:367
  181.7 1.7 collective-permute-start.47
  (118 shorter events, 27.5 us)
Async XLA Ops:
  4.7 10.3 %collective-permute-start = (f32[327]{0:T(512)S(1)}, f32[327]{0:T(512)S(1)}, u32[]{:S(2)}, u32[]{:S(2)}) collective-permute-start(f32[327]{0:T(512)S(1)} %pad_maximum_fusion.2), channel_id=1, source_target_pairs={{0,1},{1,0},{2,3},{3,2},{4,5},{5,4},{6,7},{7,6},{8,9},{9,8},{10,11... | collective-permute-start | bytes 3932 | tf_op jit(solution)/shard_map/ppermute | solution.py:371
  6.1 26.0 %collective-permute-start.1 = (f32[15,64,128]{2,1,0:T(8,128)}, f32[15,64,128]{2,1,0:T(8,128)S(1)}, u32[]{:S(2)}, u32[]{:S(2)}) collective-permute-start(f32[15,64,128]{2,1,0:T(8,128)} %get-tuple-element.114), channel_id=1, source_target_pairs={{2,4},{4,2},{6,8},{8,6},{10,12},{12,10},{14,16},{16,14},{18,20},{2... | collective-permute-start | bytes 1474568 | tf_op jit(solution)/shard_map/ppermute | solution.py:367
  14.6 17.6 %collective-permute-start.2 = (f32[15,64,128]{2,1,0:T(8,128)}, f32[15,64,128]{2,1,0:T(8,128)S(1)}, u32[]{:S(2)}, u32[]{:S(2)}) collective-permute-start(f32[15,64,128]{2,1,0:T(8,128)} %get-tuple-element.115), channel_id=1, source_target_pairs={{0,2},{2,0},{4,6},{6,4},{8,10},{10,8},{12,14},{14,12},{16,18},{18,... | collective-permute-start | bytes 1474568 | tf_op jit(solution)/shard_map/ppermute | solution.py:367
  14.6 20.8 %collective-permute-start.4 = (f32[16,64,128]{2,1,0:T(8,128)S(1)}, f32[16,64,128]{2,1,0:T(8,128)S(1)}, u32[]{:S(2)}, u32[]{:S(2)}) collective-permute-start(f32[16,64,128]{2,1,0:T(8,128)S(1)} %get-tuple-element.113.own), channel_id=1, source_target_pairs={{0,1},{1,0},{2,3},{3,2},{4,5},{5,4},{6,7},{7,6},{8,9},{9,8},{10,11... | collective-permute-start | bytes 1572872 | tf_op jit(solution)/shard_map/ppermute | solution.py:371
  15.1 14.6 %collective-permute-start.7 = (f32[96]{0:T(128)S(1)}, f32[96]{0:T(128)S(1)}, u32[]{:S(2)}, u32[]{:S(2)}) collective-permute-start(f32[96]{0:T(128)S(1)} %pad_maximum_fusion.4), channel_id=1, source_target_pairs={{0,2},{2,4},{4,6},{6,8},{8,10},{10,12},{12,14},{14,16},{16,18},{18... | collective-permute-start | bytes 1160 | tf_op jit(solution)/shard_map/ppermute | solution.py:390
  16.9 12.9 %collective-permute-start.8 = (f32[96]{0:T(128)S(1)}, f32[96]{0:T(128)S(1)}, u32[]{:S(2)}, u32[]{:S(2)}) collective-permute-start(f32[96]{0:T(128)S(1)} %pad_maximum_fusion.4), channel_id=1, source_target_pairs={{2,0},{4,2},{6,4},{8,6},{10,8},{12,10},{14,12},{16,14},{18,16},{20... | collective-permute-start | bytes 1160 | tf_op jit(solution)/shard_map/ppermute | solution.py:391
  29.8 7.1 %collective-permute-start.6 = (f32[3,16,80,128]{3,2,1,0:T(8,128)S(1)}, f32[3,16,80,128]{3,2,1,0:T(8,128)S(1)}, u32[]{:S(2)}, u32[]{:S(2)}) collective-permute-start(f32[3,16,80,128]{3,2,1,0:T(8,128)S(1)} %get-tuple-element.126), channel_id=1, source_target_pairs={{0,1},{1,0},{2,3},{3,2},{4,5},{5,4},{6,7},{7,6},{8,9},{9,8},{10,11... | collective-permute-start | bytes 5898248 | tf_op jit(solution)/shard_map/ppermute | solution.py:371
  32.1 3.3 %collective-permute-start.3 = (f32[15,64,128]{2,1,0:T(8,128)S(1)}, f32[15,64,128]{2,1,0:T(8,128)S(1)}, u32[]{:S(2)}, u32[]{:S(2)}) collective-permute-start(f32[15,64,128]{2,1,0:T(8,128)S(1)} %collective-permute-done.1.first), channel_id=1, source_target_pairs={{0,1},{1,0},{2,3},{3,2},{4,5},{5,4},{6,7},{7,6},{8,9},{9,8},{10,11... | collective-permute-start | bytes 1474568 | tf_op jit(solution)/shard_map/ppermute | solution.py:371
  32.2 3.3 %collective-permute-start.5 = (f32[15,64,128]{2,1,0:T(8,128)S(1)}, f32[15,64,128]{2,1,0:T(8,128)S(1)}, u32[]{:S(2)}, u32[]{:S(2)}) collective-permute-start(f32[15,64,128]{2,1,0:T(8,128)S(1)} %collective-permute-done.2.second), channel_id=1, source_target_pairs={{0,1},{1,0},{2,3},{3,2},{4,5},{5,4},{6,7},{7,6},{8,9},{9,8},{10,11... | collective-permute-start | bytes 1474568 | tf_op jit(solution)/shard_map/ppermute | solution.py:371
  43.8 12.8 %collective-permute-start.11 = (f32[15,32,128]{2,1,0:T(8,128)}, f32[15,32,128]{2,1,0:T(8,128)S(1)}, u32[]{:S(2)}, u32[]{:S(2)}) collective-permute-start(f32[15,32,128]{2,1,0:T(8,128)} %get-tuple-element.134), channel_id=1, source_target_pairs={{2,4},{4,2},{6,8},{8,6},{10,12},{12,10},{14,16},{16,14},{18,20},{2... | collective-permute-start | bytes 737288 | tf_op jit(solution)/shard_map/ppermute | solution.py:367
  47.3 9.3 %collective-permute-start.12 = (f32[15,32,128]{2,1,0:T(8,128)}, f32[15,32,128]{2,1,0:T(8,128)S(1)}, u32[]{:S(2)}, u32[]{:S(2)}) collective-permute-start(f32[15,32,128]{2,1,0:T(8,128)} %get-tuple-element.135), channel_id=1, source_target_pairs={{0,2},{2,0},{4,6},{6,4},{8,10},{10,8},{12,14},{14,12},{16,18},{18,... | collective-permute-start | bytes 737288 | tf_op jit(solution)/shard_map/ppermute | solution.py:367
  47.4 13.5 %collective-permute-start.10 = (f32[15,32,128]{2,1,0:T(8,128)}, f32[15,32,128]{2,1,0:T(8,128)S(1)}, u32[]{:S(2)}, u32[]{:S(2)}) collective-permute-start(f32[15,32,128]{2,1,0:T(8,128)} %copy-done.8), channel_id=1, source_target_pairs={{0,2},{2,0},{4,6},{6,4},{8,10},{10,8},{12,14},{14,12},{16,18},{18,... | collective-permute-start | bytes 737288 | tf_op jit(solution)/shard_map/ppermute | solution.py:367
  48.9 12.3 %collective-permute-start.9 = (f32[15,32,128]{2,1,0:T(8,128)S(1)}, f32[15,32,128]{2,1,0:T(8,128)S(1)}, u32[]{:S(2)}, u32[]{:S(2)}) collective-permute-start(f32[15,32,128]{2,1,0:T(8,128)S(1)} %get-tuple-element.131), channel_id=1, source_target_pairs={{2,4},{4,2},{6,8},{8,6},{10,12},{12,10},{14,16},{16,14},{18,20},{2... | collective-permute-start | bytes 737288 | tf_op jit(solution)/shard_map/ppermute | solution.py:367
  57.3 11.5 %collective-permute-start.13 = (f32[15,32,128]{2,1,0:T(8,128)S(1)}, f32[15,32,128]{2,1,0:T(8,128)S(1)}, u32[]{:S(2)}, u32[]{:S(2)}) collective-permute-start(f32[15,32,128]{2,1,0:T(8,128)S(1)} %get-tuple-element.140), channel_id=1, source_target_pairs={{2,4},{4,2},{6,8},{8,6},{10,12},{12,10},{14,16},{16,14},{18,20},{2... | collective-permute-start | bytes 737288 | tf_op jit(solution)/shard_map/ppermute | solution.py:367
  60.9 10.3 %collective-permute-start.16 = (f32[15,32,128]{2,1,0:T(8,128)S(1)}, f32[15,32,128]{2,1,0:T(8,128)S(1)}, u32[]{:S(2)}, u32[]{:S(2)}) collective-permute-start(f32[15,32,128]{2,1,0:T(8,128)S(1)} %get-tuple-element.142), channel_id=1, source_target_pairs={{0,2},{2,0},{4,6},{6,4},{8,10},{10,8},{12,14},{14,12},{16,18},{18,... | collective-permute-start | bytes 737288 | tf_op jit(solution)/shard_map/ppermute | solution.py:367
  61.2 11.3 %collective-permute-start.15 = (f32[16,32,128]{2,1,0:T(8,128)S(1)}, f32[16,32,128]{2,1,0:T(8,128)S(1)}, u32[]{:S(2)}, u32[]{:S(2)}) collective-permute-start(f32[16,32,128]{2,1,0:T(8,128)S(1)} %get-tuple-element.141.own.current), channel_id=1, source_target_pairs={{0,1},{1,0},{2,3},{3,2},{4,5},{5,4},{6,7},{7,6},{8,9},{9,8},{10,11... | collective-permute-start | bytes 786440 | tf_op jit(solution)/shard_map/ppermute | solution.py:371
  63.8 13.1 %collective-permute-start.18 = (f32[15,32,128]{2,1,0:T(8,128)S(1)}, f32[15,32,128]{2,1,0:T(8,128)S(1)}, u32[]{:S(2)}, u32[]{:S(2)}) collective-permute-start(f32[15,32,128]{2,1,0:T(8,128)S(1)} %get-tuple-element.148), channel_id=1, source_target_pairs={{2,4},{4,2},{6,8},{8,6},{10,12},{12,10},{14,16},{16,14},{18,20},{2... | collective-permute-start | bytes 737288 | tf_op jit(solution)/shard_map/ppermute | solution.py:367
  67.3 9.5 %collective-permute-start.19 = (f32[15,32,128]{2,1,0:T(8,128)S(1)}, f32[15,32,128]{2,1,0:T(8,128)S(1)}, u32[]{:S(2)}, u32[]{:S(2)}) collective-permute-start(f32[15,32,128]{2,1,0:T(8,128)S(1)} %get-tuple-element.149), channel_id=1, source_target_pairs={{0,2},{2,0},{4,6},{6,4},{8,10},{10,8},{12,14},{14,12},{16,18},{18,... | collective-permute-start | bytes 737288 | tf_op jit(solution)/shard_map/ppermute | solution.py:367
  68.8 3.7 %collective-permute-start.14 = (f32[15,32,128]{2,1,0:T(8,128)S(1)}, f32[15,32,128]{2,1,0:T(8,128)S(1)}, u32[]{:S(2)}, u32[]{:S(2)}) collective-permute-start(f32[15,32,128]{2,1,0:T(8,128)S(1)} %collective-permute-done.13.first), channel_id=1, source_target_pairs={{0,1},{1,0},{2,3},{3,2},{4,5},{5,4},{6,7},{7,6},{8,9},{9,8},{10,11... | collective-permute-start | bytes 737288 | tf_op jit(solution)/shard_map/ppermute | solution.py:371
  71.2 1.5 collective-permute-start.17
  83.7 12.2 %collective-permute-start.22 = (f32[15,32,128]{2,1,0:T(8,128)S(1)}, f32[15,32,128]{2,1,0:T(8,128)S(1)}, u32[]{:S(2)}, u32[]{:S(2)}) collective-permute-start(f32[15,32,128]{2,1,0:T(8,128)S(1)} %get-tuple-element.158), channel_id=1, source_target_pairs={{2,4},{4,2},{6,8},{8,6},{10,12},{12,10},{14,16},{16,14},{18,20},{2... | collective-permute-start | bytes 737288 | tf_op jit(solution)/shard_map/ppermute | solution.py:367
  87.2 8.6 %collective-permute-start.23 = (f32[15,32,128]{2,1,0:T(8,128)S(1)}, f32[15,32,128]{2,1,0:T(8,128)S(1)}, u32[]{:S(2)}, u32[]{:S(2)}) collective-permute-start(f32[15,32,128]{2,1,0:T(8,128)S(1)} %get-tuple-element.159), channel_id=1, source_target_pairs={{0,2},{2,0},{4,6},{6,4},{8,10},{10,8},{12,14},{14,12},{16,18},{18,... | collective-permute-start | bytes 737288 | tf_op jit(solution)/shard_map/ppermute | solution.py:367
  87.2 13.9 %collective-permute-start.20 = (f32[15,32,128]{2,1,0:T(8,128)S(1)}, f32[15,32,128]{2,1,0:T(8,128)S(1)}, u32[]{:S(2)}, u32[]{:S(2)}) collective-permute-start(f32[15,32,128]{2,1,0:T(8,128)S(1)} %get-tuple-element.155), channel_id=1, source_target_pairs={{2,4},{4,2},{6,8},{8,6},{10,12},{12,10},{14,16},{16,14},{18,20},{2... | collective-permute-start | bytes 737288 | tf_op jit(solution)/shard_map/ppermute | solution.py:367
  90.6 10.5 %collective-permute-start.21 = (f32[15,32,128]{2,1,0:T(8,128)S(1)}, f32[15,32,128]{2,1,0:T(8,128)S(1)}, u32[]{:S(2)}, u32[]{:S(2)}) collective-permute-start(f32[15,32,128]{2,1,0:T(8,128)S(1)} %get-tuple-element.156), channel_id=1, source_target_pairs={{0,2},{2,0},{4,6},{6,4},{8,10},{10,8},{12,14},{14,12},{16,18},{18,... | collective-permute-start | bytes 737288 | tf_op jit(solution)/shard_map/ppermute | solution.py:367
  96.6 11.1 %collective-permute-start.24 = (f32[15,32,128]{2,1,0:T(8,128)S(1)}, f32[15,32,128]{2,1,0:T(8,128)S(1)}, u32[]{:S(2)}, u32[]{:S(2)}) collective-permute-start(f32[15,32,128]{2,1,0:T(8,128)S(1)} %get-tuple-element.164), channel_id=1, source_target_pairs={{2,4},{4,2},{6,8},{8,6},{10,12},{12,10},{14,16},{16,14},{18,20},{2... | collective-permute-start | bytes 737288 | tf_op jit(solution)/shard_map/ppermute | solution.py:367
  100.1 11.1 %collective-permute-start.27 = (f32[15,32,128]{2,1,0:T(8,128)S(1)}, f32[15,32,128]{2,1,0:T(8,128)S(1)}, u32[]{:S(2)}, u32[]{:S(2)}) collective-permute-start(f32[15,32,128]{2,1,0:T(8,128)S(1)} %get-tuple-element.166), channel_id=1, source_target_pairs={{0,2},{2,0},{4,6},{6,4},{8,10},{10,8},{12,14},{14,12},{16,18},{18,... | collective-permute-start | bytes 737288 | tf_op jit(solution)/shard_map/ppermute | solution.py:367
  101.1 11.5 %collective-permute-start.26 = (f32[16,32,128]{2,1,0:T(8,128)S(1)}, f32[16,32,128]{2,1,0:T(8,128)S(1)}, u32[]{:S(2)}, u32[]{:S(2)}) collective-permute-start(f32[16,32,128]{2,1,0:T(8,128)S(1)} %get-tuple-element.165.own.current), channel_id=1, source_target_pairs={{0,1},{1,0},{2,3},{3,2},{4,5},{5,4},{6,7},{7,6},{8,9},{9,8},{10,11... | collective-permute-start | bytes 786440 | tf_op jit(solution)/shard_map/ppermute | solution.py:371
  104.2 13.1 %collective-permute-start.29 = (f32[15,32,128]{2,1,0:T(8,128)S(1)}, f32[15,32,128]{2,1,0:T(8,128)S(1)}, u32[]{:S(2)}, u32[]{:S(2)}) collective-permute-start(f32[15,32,128]{2,1,0:T(8,128)S(1)} %get-tuple-element.172), channel_id=1, source_target_pairs={{2,4},{4,2},{6,8},{8,6},{10,12},{12,10},{14,16},{16,14},{18,20},{2... | collective-permute-start | bytes 737288 | tf_op jit(solution)/shard_map/ppermute | solution.py:367
  107.6 9.6 %collective-permute-start.30 = (f32[15,32,128]{2,1,0:T(8,128)S(1)}, f32[15,32,128]{2,1,0:T(8,128)S(1)}, u32[]{:S(2)}, u32[]{:S(2)}) collective-permute-start(f32[15,32,128]{2,1,0:T(8,128)S(1)} %get-tuple-element.173), channel_id=1, source_target_pairs={{0,2},{2,0},{4,6},{6,4},{8,10},{10,8},{12,14},{14,12},{16,18},{18,... | collective-permute-start | bytes 737288 | tf_op jit(solution)/shard_map/ppermute | solution.py:367
  107.6 5.0 %collective-permute-start.25 = (f32[15,32,128]{2,1,0:T(8,128)S(1)}, f32[15,32,128]{2,1,0:T(8,128)S(1)}, u32[]{:S(2)}, u32[]{:S(2)}) collective-permute-start(f32[15,32,128]{2,1,0:T(8,128)S(1)} %collective-permute-done.24.first), channel_id=1, source_target_pairs={{0,1},{1,0},{2,3},{3,2},{4,5},{5,4},{6,7},{7,6},{8,9},{9,8},{10,11... | collective-permute-start | bytes 737288 | tf_op jit(solution)/shard_map/ppermute | solution.py:371
  111.2 1.5 collective-permute-start.28
  124.0 12.2 %collective-permute-start.33 = (f32[15,32,128]{2,1,0:T(8,128)S(1)}, f32[15,32,128]{2,1,0:T(8,128)S(1)}, u32[]{:S(2)}, u32[]{:S(2)}) collective-permute-start(f32[15,32,128]{2,1,0:T(8,128)S(1)} %get-tuple-element.182), channel_id=1, source_target_pairs={{2,4},{4,2},{6,8},{8,6},{10,12},{12,10},{14,16},{16,14},{18,20},{2... | collective-permute-start | bytes 737288 | tf_op jit(solution)/shard_map/ppermute | solution.py:367
  127.5 8.7 %collective-permute-start.34 = (f32[15,32,128]{2,1,0:T(8,128)S(1)}, f32[15,32,128]{2,1,0:T(8,128)S(1)}, u32[]{:S(2)}, u32[]{:S(2)}) collective-permute-start(f32[15,32,128]{2,1,0:T(8,128)S(1)} %get-tuple-element.183), channel_id=1, source_target_pairs={{0,2},{2,0},{4,6},{6,4},{8,10},{10,8},{12,14},{14,12},{16,18},{18,... | collective-permute-start | bytes 737288 | tf_op jit(solution)/shard_map/ppermute | solution.py:367
  127.5 14.0 %collective-permute-start.31 = (f32[15,32,128]{2,1,0:T(8,128)S(1)}, f32[15,32,128]{2,1,0:T(8,128)S(1)}, u32[]{:S(2)}, u32[]{:S(2)}) collective-permute-start(f32[15,32,128]{2,1,0:T(8,128)S(1)} %get-tuple-element.179), channel_id=1, source_target_pairs={{2,4},{4,2},{6,8},{8,6},{10,12},{12,10},{14,16},{16,14},{18,20},{2... | collective-permute-start | bytes 737288 | tf_op jit(solution)/shard_map/ppermute | solution.py:367
  131.0 10.5 %collective-permute-start.32 = (f32[15,32,128]{2,1,0:T(8,128)S(1)}, f32[15,32,128]{2,1,0:T(8,128)S(1)}, u32[]{:S(2)}, u32[]{:S(2)}) collective-permute-start(f32[15,32,128]{2,1,0:T(8,128)S(1)} %get-tuple-element.180), channel_id=1, source_target_pairs={{0,2},{2,0},{4,6},{6,4},{8,10},{10,8},{12,14},{14,12},{16,18},{18,... | collective-permute-start | bytes 737288 | tf_op jit(solution)/shard_map/ppermute | solution.py:367
  136.9 11.1 %collective-permute-start.35 = (f32[15,32,128]{2,1,0:T(8,128)S(1)}, f32[15,32,128]{2,1,0:T(8,128)S(1)}, u32[]{:S(2)}, u32[]{:S(2)}) collective-permute-start(f32[15,32,128]{2,1,0:T(8,128)S(1)} %get-tuple-element.188), channel_id=1, source_target_pairs={{2,4},{4,2},{6,8},{8,6},{10,12},{12,10},{14,16},{16,14},{18,20},{2... | collective-permute-start | bytes 737288 | tf_op jit(solution)/shard_map/ppermute | solution.py:367
  140.4 11.2 %collective-permute-start.38 = (f32[15,32,128]{2,1,0:T(8,128)S(1)}, f32[15,32,128]{2,1,0:T(8,128)S(1)}, u32[]{:S(2)}, u32[]{:S(2)}) collective-permute-start(f32[15,32,128]{2,1,0:T(8,128)S(1)} %get-tuple-element.190), channel_id=1, source_target_pairs={{0,2},{2,0},{4,6},{6,4},{8,10},{10,8},{12,14},{14,12},{16,18},{18,... | collective-permute-start | bytes 737288 | tf_op jit(solution)/shard_map/ppermute | solution.py:367
  141.4 11.5 %collective-permute-start.37 = (f32[16,32,128]{2,1,0:T(8,128)S(1)}, f32[16,32,128]{2,1,0:T(8,128)S(1)}, u32[]{:S(2)}, u32[]{:S(2)}) collective-permute-start(f32[16,32,128]{2,1,0:T(8,128)S(1)} %get-tuple-element.189.own.current), channel_id=1, source_target_pairs={{0,1},{1,0},{2,3},{3,2},{4,5},{5,4},{6,7},{7,6},{8,9},{9,8},{10,11... | collective-permute-start | bytes 786440 | tf_op jit(solution)/shard_map/ppermute | solution.py:371
  144.4 13.1 %collective-permute-start.40 = (f32[15,32,128]{2,1,0:T(8,128)S(1)}, f32[15,32,128]{2,1,0:T(8,128)S(1)}, u32[]{:S(2)}, u32[]{:S(2)}) collective-permute-start(f32[15,32,128]{2,1,0:T(8,128)S(1)} %get-tuple-element.196), channel_id=1, source_target_pairs={{2,4},{4,2},{6,8},{8,6},{10,12},{12,10},{14,16},{16,14},{18,20},{2... | collective-permute-start | bytes 737288 | tf_op jit(solution)/shard_map/ppermute | solution.py:367
  148.0 9.5 %collective-permute-start.41 = (f32[15,32,128]{2,1,0:T(8,128)S(1)}, f32[15,32,128]{2,1,0:T(8,128)S(1)}, u32[]{:S(2)}, u32[]{:S(2)}) collective-permute-start(f32[15,32,128]{2,1,0:T(8,128)S(1)} %get-tuple-element.197), channel_id=1, source_target_pairs={{0,2},{2,0},{4,6},{6,4},{8,10},{10,8},{12,14},{14,12},{16,18},{18,... | collective-permute-start | bytes 737288 | tf_op jit(solution)/shard_map/ppermute | solution.py:367
  148.0 4.9 %collective-permute-start.36 = (f32[15,32,128]{2,1,0:T(8,128)S(1)}, f32[15,32,128]{2,1,0:T(8,128)S(1)}, u32[]{:S(2)}, u32[]{:S(2)}) collective-permute-start(f32[15,32,128]{2,1,0:T(8,128)S(1)} %collective-permute-done.35.first), channel_id=1, source_target_pairs={{0,1},{1,0},{2,3},{3,2},{4,5},{5,4},{6,7},{7,6},{8,9},{9,8},{10,11... | collective-permute-start | bytes 737288 | tf_op jit(solution)/shard_map/ppermute | solution.py:371
  151.6 1.5 collective-permute-start.39
  164.2 12.2 %collective-permute-start.44 = (f32[15,32,128]{2,1,0:T(8,128)S(1)}, f32[15,32,128]{2,1,0:T(8,128)S(1)}, u32[]{:S(2)}, u32[]{:S(2)}) collective-permute-start(f32[15,32,128]{2,1,0:T(8,128)S(1)} %get-tuple-element.206), channel_id=1, source_target_pairs={{2,4},{4,2},{6,8},{8,6},{10,12},{12,10},{14,16},{16,14},{18,20},{2... | collective-permute-start | bytes 737288 | tf_op jit(solution)/shard_map/ppermute | solution.py:367
  167.8 8.6 %collective-permute-start.45 = (f32[15,32,128]{2,1,0:T(8,128)S(1)}, f32[15,32,128]{2,1,0:T(8,128)S(1)}, u32[]{:S(2)}, u32[]{:S(2)}) collective-permute-start(f32[15,32,128]{2,1,0:T(8,128)S(1)} %get-tuple-element.207), channel_id=1, source_target_pairs={{0,2},{2,0},{4,6},{6,4},{8,10},{10,8},{12,14},{14,12},{16,18},{18,... | collective-permute-start | bytes 737288 | tf_op jit(solution)/shard_map/ppermute | solution.py:367
  167.8 13.9 %collective-permute-start.42 = (f32[15,32,128]{2,1,0:T(8,128)S(1)}, f32[15,32,128]{2,1,0:T(8,128)S(1)}, u32[]{:S(2)}, u32[]{:S(2)}) collective-permute-start(f32[15,32,128]{2,1,0:T(8,128)S(1)} %get-tuple-element.203), channel_id=1, source_target_pairs={{2,4},{4,2},{6,8},{8,6},{10,12},{12,10},{14,16},{16,14},{18,20},{2... | collective-permute-start | bytes 737288 | tf_op jit(solution)/shard_map/ppermute | solution.py:367
  171.2 10.5 %collective-permute-start.43 = (f32[15,32,128]{2,1,0:T(8,128)S(1)}, f32[15,32,128]{2,1,0:T(8,128)S(1)}, u32[]{:S(2)}, u32[]{:S(2)}) collective-permute-start(f32[15,32,128]{2,1,0:T(8,128)S(1)} %get-tuple-element.204), channel_id=1, source_target_pairs={{0,2},{2,0},{4,6},{6,4},{8,10},{10,8},{12,14},{14,12},{16,18},{18,... | collective-permute-start | bytes 737288 | tf_op jit(solution)/shard_map/ppermute | solution.py:367
  181.7 2.9 %collective-permute-start.47 = (f32[16,32,128]{2,1,0:T(8,128)S(1)}, f32[16,32,128]{2,1,0:T(8,128)S(1)}, u32[]{:S(2)}, u32[]{:S(2)}) collective-permute-start(f32[16,32,128]{2,1,0:T(8,128)S(1)} %update.14), channel_id=1, source_target_pairs={{0,1},{1,0},{2,3},{3,2},{4,5},{5,4},{6,7},{7,6},{8,9},{9,8},{10,11... | collective-permute-start | bytes 786440 | tf_op jit(solution)/shard_map/ppermute | solution.py:371
  184.1 1.6 collective-permute-start.46
  (12 other events, 60.4 us)
